TPU v7x, 128 devices: a whole 4x4x4 slice. The times are simulated.
128 devices in a mesh: rows: 16 (over z_lo, y, core), layers: 8 (over x, z_hi).
Axes of the slice: x: 4, y: 4, z: 4 (z_hi: 2, z_lo: 2; z = z_hi * 2 + z_lo), core: 2. Of those that a mesh axis runs over, the one named last changes fastest.
Arguments:
- queries: bfloat16 [1024, 16, 4096], P('rows', 'layers'), may hold values from -40 to 40
- stored_rows: bfloat16 [16384, 16, 4096], P('rows', 'layers'), may hold values from -6 to 6
- left_inverse: float32 [16, 64, 64], P('layers'), may hold values from -1 to 24
- right_inverse: float32 [16, 64, 64], P('layers'), may hold values from -1 to 24
Outputs:
- scores: float32 [1024, 16384], P('layers', 'rows')
All inputs are finite; a program needn't handle non-finite values.
Results may differ from a plain program's by a relative error of at most 0.0029.
Values may be sent and summed in bfloat16 or wider, within the bound.
No kernel may reach another device: no remote copies, remote signals or barrier semaphores. Data moves between devices by JAX's collectives and lax.ppermute only.
A program may use at most 192 MiB of HBM per device.

v0:
```python
import functools

import jax
import jax.numpy as jnp
from jax import lax
from jax.experimental import pallas as pl
from jax.experimental.pallas import tpu as pltpu
from jax.sharding import PartitionSpec as P

EPS = 1e-06
BF = jnp.bfloat16
F32 = jnp.float32
PAD = 128
MIB = 1 << 20

Z, Y, C, X, ZH = 2, 4, 2, 4, 2
BOTH = ("rows", "layers")


def rows_index(z, y, c):
    return (z * Y + y % Y) * C + c


def rows_perm(move):
    pairs = []
    for z in range(Z):
        for y in range(Y):
            for c in range(C):
                pairs.append((rows_index(z, y, c), rows_index(*move(z, y, c))))
    return pairs


SAME = rows_perm(lambda z, y, c: (z, y ^ 1, c))
OPPOSITE = rows_perm(lambda z, y, c: (z, y - 1 if y % 2 == 0 else y + 1, c))
ACROSS = rows_perm(lambda z, y, c: (1 - z, y, c))
SIBLING = rows_perm(lambda z, y, c: (z, y, 1 - c))


def whole_perm(move):
    pairs = []
    for z in range(Z):
        for y in range(Y):
            for c in range(C):
                for x in range(X):
                    for zh in range(ZH):
                        to = move(z, y, x, zh)
                        if to is not None:
                            r = rows_index(z, y, c)
                            source = r * X * ZH + x * ZH + zh
                            target = r * X * ZH + (to[0] % X) * ZH + to[1]
                            pairs.append((source, target))
    return pairs


def norm_columns(norms):
    count = norms.shape[0]
    high = norms.astype(BF).astype(F32)
    low = norms - high
    lane = lax.broadcasted_iota(jnp.int32, (count, PAD), 1)
    return jnp.where(lane < PAD // 2, high, low).astype(BF)


def thirds(value):
    parts = []
    for _ in range(3):
        parts.append(value.astype(BF))
        value = value - parts[-1].astype(F32)
    return parts

def dot(a, b):
    return lax.dot_general(a, b, (((1,), (0,)), ((), ())), preferred_element_type=F32)

def condition_kernel(q, left, right, out, swapped, back, turned_left):
    count, layers, width = q.shape
    side = right.shape[1]
    four = 4 * side
    tiles = width // 128
    row = lax.broadcasted_iota(jnp.int32, (four, four), 0)
    col = lax.broadcasted_iota(jnp.int32, (four, four), 1)
    right_mask = row // side == col // side
    left_mask = row % 128 // 32 == col % 128 // 32
    total = jnp.zeros((count, 128), F32)
    for l in range(layers):
        lanes = jnp.concatenate([right[l]] * 4, axis=1)
        wide_r = jnp.where(right_mask, jnp.concatenate([lanes] * 4, axis=0), 0.0)
        x = q[:, l, :]
        rows = jnp.concatenate([x[:, four * g : four * (g + 1)] for g in range(width // four)], axis=0)
        first = sum(dot(rows, part) for part in reversed(thirds(wide_r)))
        for g in range(width // four):
            for h in range(four // 128):
                swapped[g * (four // 128) + h] = first[count * g : count * (g + 1), 128 * h : 128 * (h + 1)]
        half = side // 2
        def halves(slot):
            return [turned_left[slot, pl.ds(i, half, stride=2), :] for i in range(2)]

        turned_left[0] = jnp.concatenate([left[l]] * 2, axis=1)
        low, high = halves(0)
        turn = jnp.concatenate([low] * 4 + [high] * 4, axis=0).T[:side]
        turned_left[1] = turn[:, :128]
        turned_left[2] = turn[:, 128:]
        low, high = (jnp.concatenate(pair, axis=1) for pair in zip(halves(1), halves(2)))
        wide_l = jnp.where(left_mask, jnp.concatenate([low] * 4 + [high] * 4, axis=0), 0.0)
        stack = []
        for j in range(count // 4):
            block = jnp.concatenate([swapped[:, 4 * j + i, :] for i in range(4)], axis=0).T
            stack.append(jnp.concatenate([block[:side], block[side:]], axis=1))
        turned = thirds(jnp.concatenate(stack, axis=0))
        factor = thirds(wide_l)
        second = dot(turned[1], factor[1]) + dot(turned[0], factor[2]) + dot(turned[2], factor[0])
        second = second + (dot(turned[0], factor[1]) + dot(turned[1], factor[0]))
        second = second + dot(turned[0], factor[0])
        for j in range(count // 4):
            piece = second[side * j : side * (j + 1)]
            block = jnp.concatenate([piece[:, :128], piece[:, 128:]], axis=0).T
            for i in range(4):
                back[4 * j + i] = block[32 * i : 32 * (i + 1)]
        for t in range(tiles):
            done = back[:, t, :].astype(BF)
            out[:, l * width + 128 * t : l * width + 128 * (t + 1)] = done
            wide = done.astype(F32)
            total = total + wide * wide
    out[:, layers * width :] = norm_columns(jnp.sum(total, axis=1, keepdims=True))

def condition(q, left, right, first, count):
    _, layers, width = q.shape
    return pl.pallas_call(
        condition_kernel,
        out_shape=jax.ShapeDtypeStruct((count, layers * width + PAD), BF),
        grid=(1,),
        in_specs=[pl.BlockSpec((count, layers, width), lambda i: (first, 0, 0)),
            pl.BlockSpec(left.shape, lambda i: (0, 0, 0)), pl.BlockSpec(right.shape, lambda i: (0, 0, 0))],
        out_specs=pl.BlockSpec((count, layers * width + PAD), lambda i: (0, 0)),
        scratch_shapes=[pltpu.VMEM((width // 128, count, 128), F32), pltpu.VMEM((count, width // 128, 128), F32), pltpu.VMEM((3, left.shape[1], 128), F32)],
        compiler_params=pltpu.CompilerParams(vmem_limit_bytes=24 * MIB),
        name="condition",
    )(q, left, right)

def fill(at, place, pieces, group):
    for i, piece in enumerate(pieces):
        rows = piece.shape[0]
        group[pl.ds(pl.multiple_of(place[at + i], 16), rows), :] = piece[...]


def products(group, stored):
    width = stored.shape[1]
    return lax.dot_general(
        group[:, :width], stored[...], (((1,), (1,)), ((), ())), preferred_element_type=F32
    )


def score_kernel(at, place, *refs):
    *pieces, stored, scores, group = refs
    edge = scores.shape[1] - PAD
    fill(at, place, pieces, group)
    scores[:, :edge] = products(group, stored).astype(BF)
    scores[:, edge:] = group[:, stored.shape[1] :]


def deal_kernel(at, deal, place, *refs):
    *pieces, stored, before, o0, o1, o2, o3, group, blocks = refs
    edge = before.shape[1] - PAD
    rows = before.shape[0]
    fill(at, place, pieces, group)
    blocks[:rows] = before[...]
    blocks[rows:, :edge] = products(group, stored).astype(BF)
    blocks[rows:, edge:] = group[:, stored.shape[1] :]
    for j, out in enumerate((o0, o1, o2, o3)):
        start = pl.multiple_of(place[deal + j] * out.shape[0], 128)
        out[...] = blocks[pl.ds(start, out.shape[0]), :]


def score_group(place, at, pieces, stored, before=None, deal=None):
    count, width = stored.shape
    rows = sum(p.shape[0] for p in pieces)
    vmem = pl.BlockSpec(memory_space=pltpu.VMEM)
    scratch = [pltpu.VMEM((rows, width + PAD), BF)]
    shape = jax.ShapeDtypeStruct((rows, count + PAD), BF)
    more = []
    if before is None:
        kernel, name = functools.partial(score_kernel, at), "score_group"
        out, out_specs = shape, vmem
    else:
        kernel, name = functools.partial(deal_kernel, at, deal), "score_and_deal"
        out = [jax.ShapeDtypeStruct((rows // 2, count + PAD), BF)] * 4
        out_specs = [vmem] * 4
        scratch.append(pltpu.VMEM((2 * rows, count + PAD), BF))
        more = [before]
    return pl.pallas_call(
        kernel,
        out_shape=out,
        in_specs=[pl.BlockSpec(memory_space=pltpu.SMEM)] + [vmem] * (len(pieces) + 1 + len(more)),
        out_specs=out_specs,
        scratch_shapes=scratch,
        compiler_params=pltpu.CompilerParams(vmem_limit_bytes=12 * MIB),
        cost_estimate=pl.CostEstimate(
            flops=2 * rows * width * count, bytes_accessed=2 * count * width, transcendentals=0
        ),
        name=name,
    )(place, *pieces, stored, *more)


def sum_kernel(v, a, b, c, keep, onward):
    edge = v.shape[1] - PAD
    total = v[...].astype(F32) + a[...].astype(F32) + b[...].astype(F32) + c[...].astype(F32)
    norms = total[:, edge : edge + 1] + total[:, edge + PAD // 2 : edge + PAD // 2 + 1]
    keep[:, :edge] = total[:, :edge]
    keep[:, edge:] = jnp.broadcast_to(norms, (v.shape[0], PAD))
    onward[:, :edge] = total[:, :edge].astype(BF)
    onward[:, edge:] = norm_columns(norms)


def sum_blocks(blocks):
    shape = blocks[0].shape
    vmem = pl.BlockSpec(memory_space=pltpu.VMEM)
    return pl.pallas_call(
        sum_kernel,
        out_shape=(jax.ShapeDtypeStruct(shape, F32), jax.ShapeDtypeStruct(shape, BF)),
        in_specs=[vmem] * 4,
        out_specs=(vmem, vmem),
        compiler_params=pltpu.CompilerParams(vmem_limit_bytes=6 * MIB),
        name="sum_blocks",
    )(*blocks)


def finish_kernel(at, which, *refs):
    *blocks, out, keep, got, sems = refs
    kinds = len(blocks) // 2
    edge = out.shape[1]
    for i in range(kinds):

        @pl.when(which[at] == i)
        def _(i=i):
            one = pltpu.make_async_copy(blocks[i], keep, sems.at[0])
            two = pltpu.make_async_copy(blocks[kinds + i], got, sems.at[1])
            one.start()
            two.start()
            one.wait()
            two.wait()

    more = got[...].astype(F32)
    norms = keep[:, edge : edge + 1] + (
        more[:, edge : edge + 1] + more[:, edge + PAD // 2 : edge + PAD // 2 + 1]
    )
    out[...] = (keep[:, :edge] + more[:, :edge]) * lax.rsqrt(norms + EPS)


def finish(which, at, keeps, gots):
    rows, width = keeps[0].shape
    return pl.pallas_call(
        functools.partial(finish_kernel, at),
        out_shape=jax.ShapeDtypeStruct((rows, width - PAD), F32),
        in_specs=[pl.BlockSpec(memory_space=pltpu.SMEM)]
        + [pl.BlockSpec(memory_space=pl.ANY)] * (2 * len(keeps)),
        scratch_shapes=[
            pltpu.VMEM((rows, width), F32),
            pltpu.VMEM((rows, width), BF),
            pltpu.SemaphoreType.DMA((2,)),
        ],
        compiler_params=pltpu.CompilerParams(vmem_limit_bytes=4 * MIB),
        name="finish",
    )(which, *keeps, *gots)


def split_kernel(a, b, first, second):
    count = first.shape[0]
    first[...] = a[:count]
    second[...] = b[count:]


def split(a, b, count):
    vmem = pl.BlockSpec(memory_space=pltpu.VMEM)
    return pl.pallas_call(
        split_kernel,
        out_shape=[jax.ShapeDtypeStruct((size, a.shape[1]), a.dtype) for size in (count, b.shape[0] - count)],
        in_specs=[vmem] * 2,
        out_specs=[vmem] * 2,
        compiler_params=pltpu.CompilerParams(vmem_limit_bytes=4 * MIB),
        name="split",
    )(a, b)


def after(value, *others):
    return lax.optimization_barrier((value, *others))[0]


def per_device(queries, stored_rows, left_inverse, right_inverse):
    row_count = stored_rows.shape[0]
    width = stored_rows.shape[1] * stored_rows.shape[2]
    n = queries.shape[0]
    rows_at = lax.axis_index("rows")
    layers_at = lax.axis_index("layers")
    z, y, core = rows_at // (Y * C), (rows_at // C) % Y, rows_at % C
    x, zh = layers_at // ZH, layers_at % ZH
    side = y // 2

    def send(value, pairs, name):
        with jax.named_scope(name):
            return lax.ppermute(value, "rows", pairs)

    def whole(value, move, name):
        with jax.named_scope(name):
            return lax.ppermute(value, BOTH, whole_perm(move))

    def place(rows_of):
        offsets = []
        for at in (core, 1 - core):
            for block, rows in enumerate(rows_of):
                start = 2 * n * block + n * at
                for count in rows:
                    offsets.append(start)
                    start = start + count
        return offsets

    def dealt():
        to = [(x + step) % X for step in (0, 1, 2, 3)]
        return [2 * (t % 2 != side) + (t // 2 != z) for t in to]

    def reduce_batch(blocks, name):
        mine, up, over, down = blocks
        got = [
            whole(up, lambda zz, yy, xx, hh: (xx + 1, hh), "up" + name),
            whole(down, lambda zz, yy, xx, hh: (xx - 1, hh), "down" + name),
            whole(over, lambda zz, yy, xx, hh: (xx + 2, hh), "over" + name),
        ]
        return sum_blocks([mine, *got])

    one = ((n,), (n,))
    cut = n // 2
    tables = [place(one), place(((n,), (cut, cut))), dealt(), [(x % 2 == side) == (zh == y % 2)]]
    starts = [sum(len(t) for t in tables[:i]) for i in range(len(tables))]
    table = jnp.stack([jnp.asarray(v, jnp.int32) for t in tables for v in t])
    queries, table = lax.optimization_barrier((queries, table))

    own = condition(queries, left_inverse, right_inverse, 0, n)
    s0 = send(own, SAME, "s0")
    q0 = send(own, OPPOSITE, "q0")
    o1 = send(own, ACROSS, "o1")
    own_sib = send(own, SIBLING, "own_sib")
    stored = after(stored_rows, own).reshape(row_count, width)
    s0, q0, o1, stored = lax.optimization_barrier((s0, q0, o1, stored))
    t0 = send(q0, SAME, "t0")
    q1 = send(o1, OPPOSITE, "q1")
    s1 = send(s0, ACROSS, "s1")
    o1_sib, q0_sib, s0_sib = send(o1, SIBLING, "o1_sib"), send(q0, SIBLING, "q0_sib"), send(s0, SIBLING, "s0_sib")
    scores_o = score_group(table, starts[0], [own, o1, own_sib, o1_sib], stored)

    t0, q1, s1, scores_o = lax.optimization_barrier((t0, q1, s1, scores_o))
    first, second = split(q1, t0, cut)
    last = [send(first, SAME, "t1a"), send(second, ACROSS, "t1b")]
    q1_sib, s1_sib, t0_sib = send(q1, SIBLING, "q1_sib"), send(s1, SIBLING, "s1_sib"), send(t0, SIBLING, "t0_sib")
    dealt_1 = score_group(table, starts[0], [q0, q1, q0_sib, q1_sib], stored, scores_o, starts[2])
    *dealt_1, s1_sib, t0_sib = lax.optimization_barrier((*dealt_1, s1_sib, t0_sib))
    scores_s = score_group(table, starts[0], [after(s0, *dealt_1), s1, s0_sib, s1_sib], stored)
    last_sib = [send(after(piece, scores_s), SIBLING, "t1_sib") for piece in last]
    keep_1, onward_1 = reduce_batch(dealt_1, "_oq")
    dealt_2 = score_group(
        table, starts[1], [t0, *last, t0_sib, *last_sib], stored, scores_s, starts[2]
    )
    keep_2, onward_2 = reduce_batch(dealt_2, "_st")

    def final_first(yy, xx, hh):
        return (xx % 2 == yy // 2) == (hh == yy % 2)

    got_1 = whole(
        onward_1, lambda zz, yy, xx, hh: None if final_first(yy, xx, hh) else (xx, 1 - hh), "oq"
    )
    got_2 = whole(
        onward_2, lambda zz, yy, xx, hh: (xx, 1 - hh) if final_first(yy, xx, hh) else None, "st"
    )
    return finish(table, starts[3], [keep_2, keep_1], [got_2, got_1])


def solution(mesh):
    in_specs = (
        P("rows", "layers", None),
        P("rows", "layers", None),
        P("layers", None, None),
        P("layers", None, None),
    )
    out_specs = P("layers", "rows")
    return jax.shard_map(
        per_device, mesh=mesh, in_specs=in_specs, out_specs=out_specs, check_vma=False
    )
```

profile of v0, /device:TPU:8, one launch (start us, length us, event | category | flops | bytes accessed | tf_op | source)
XLA Modules:
  0.0 130.7 jit_solution(10071170088342846554)
XLA Ops:
  3.0 9.9 %condition.1.refs_0_ = bf16[64,8320]{1,0:T(8,128)(2,1)S(1)} custom-call(bf16[64,2,4096]{2,1,0:T(2,128)(2,1)S(1)} %copy-done, f32[2,64,64]{2,1,0:T(8,128)S(1)} %copy-done.1, f32[2,64,64]{2,1,0:T(8,128)S(1)} %copy-done.2), custom_call_target="tpu_custom_call" | custom-call | tf_op jit(solution)/shard_map/condition/pallas_call | solution.py:126
  13.3 2.5 %collective-permute-start.1 = (bf16[64,8320]{1,0:T(8,128)(2,1)S(1)}, bf16[64,8320]{1,0:T(8,128)(2,1)S(1)}, u32[]{:S(2)}, u32[]{:S(2)}) collective-permute-start(bf16[64,8320]{1,0:T(8,128)(2,1)S(1)} %condition.1.refs_0_), channel_id=1, source_target_pairs={{0,48},{8,56},{16,32},{24,40},{32,16},{40,24},{48,0},{56,8},{64,11... | collective-permute-start | bytes 3194888 | tf_op jit(solution)/shard_map/q0/ppermute | solution.py:298
  15.8 1.9 %collective-permute-start.2 = (bf16[64,8320]{1,0:T(8,128)(2,1)S(1)}, bf16[64,8320]{1,0:T(8,128)(2,1)S(1)}, u32[]{:S(2)}, u32[]{:S(2)}) collective-permute-start(bf16[64,8320]{1,0:T(8,128)(2,1)S(1)} %condition.1.refs_0_), channel_id=1, source_target_pairs={{0,64},{8,72},{16,80},{24,88},{32,96},{40,104},{48,112},{56,120},{... | collective-permute-start | bytes 3194888 | tf_op jit(solution)/shard_map/o1/ppermute | solution.py:298
  17.7 14.7 %copy.5 = bf16[128,8,2,4096]{3,1,2,0:T(8,128)(2,1)S(1)} copy(bf16[128,8,2,4096]{3,2,1,0:T(2,128)(2,1)} %bitcast.17) | data formatting | bytes 33554432
  32.4 5.8 %collective-permute-done.refs_0_ = bf16[64,8320]{1,0:T(8,128)(2,1)S(1)} collective-permute-done((bf16[64,8320]{1,0:T(8,128)(2,1)S(1)}, bf16[64,8320]{1,0:T(8,128)(2,1)S(1)}, u32[]{:S(2)}, u32[]{:S(2)}) %collective-permute-start) | collective-permute-done | bytes 1064992 | tf_op jit(solution)/shard_map/s0/ppermute | solution.py:298
  39.0 1.6 %collective-permute-done.2.refs_1_ = bf16[64,8320]{1,0:T(8,128)(2,1)S(1)} collective-permute-done((bf16[64,8320]{1,0:T(8,128)(2,1)S(1)}, bf16[64,8320]{1,0:T(8,128)(2,1)S(1)}, u32[]{:S(2)}, u32[]{:S(2)}) %collective-permute-start.2) | collective-permute-done | bytes 1064992 | tf_op jit(solution)/shard_map/o1/ppermute | solution.py:298
  40.9 2.4 %collective-permute-start.3 = (bf16[64,8320]{1,0:T(8,128)(2,1)S(1)}, bf16[64,8320]{1,0:T(8,128)(2,1)S(1)}, u32[]{:S(2)}, u32[]{:S(2)}) collective-permute-start(bf16[64,8320]{1,0:T(8,128)(2,1)S(1)} %collective-permute-done.1.refs_0_), channel_id=1, source_target_pairs={{0,16},{8,24},{16,0},{24,8},{32,48},{40,56},{48,32},{56,40},{64,80... | collective-permute-start | bytes 3194888 | tf_op jit(solution)/shard_map/t0/ppermute | solution.py:298
  43.3 1.9 %collective-permute-start.5 = (bf16[64,8320]{1,0:T(8,128)(2,1)S(1)}, bf16[64,8320]{1,0:T(8,128)(2,1)S(1)}, u32[]{:S(2)}, u32[]{:S(2)}) collective-permute-start(bf16[64,8320]{1,0:T(8,128)(2,1)S(1)} %collective-permute-done.refs_0_), channel_id=1, source_target_pairs={{0,64},{8,72},{16,80},{24,88},{32,96},{40,104},{48,112},{56,120},{... | collective-permute-start | bytes 3194888 | tf_op jit(solution)/shard_map/s1/ppermute | solution.py:298
  45.2 5.3 %score_group.2.refs_5_ = bf16[256,1152]{1,0:T(8,128)(2,1)S(1)} custom-call(s32[15]{0:T(128)S(1)} %stack.55.place.which, bf16[64,8320]{1,0:T(8,128)(2,1)S(1)} %condition.1.refs_0_, bf16[64,8320]{1,0:T(8,128)(2,1)S(1)} %collective-permute-done.2.refs_1_, bf16[64,8320]{1,0:T(8,128)(2,1)S(1)} %collective-permute-done.6.refs_2_, ...), custom_call_target="tpu_custom_call" | custom-call | flops 4294967296 | bytes 16777216 | tf_op jit(solution)/shard_map/score_group/pallas_call | solution.py:188
  50.5 16.7 %collective-permute-done.3.b.refs_0_ = bf16[64,8320]{1,0:T(8,128)(2,1)S(1)} collective-permute-done((bf16[64,8320]{1,0:T(8,128)(2,1)S(1)}, bf16[64,8320]{1,0:T(8,128)(2,1)S(1)}, u32[]{:S(2)}, u32[]{:S(2)}) %collective-permute-start.3) | collective-permute-done | bytes 1064992 | tf_op jit(solution)/shard_map/t0/ppermute | solution.py:298
  67.2 1.6 %collective-permute-done.5.refs_1_ = bf16[64,8320]{1,0:T(8,128)(2,1)S(1)} collective-permute-done((bf16[64,8320]{1,0:T(8,128)(2,1)S(1)}, bf16[64,8320]{1,0:T(8,128)(2,1)S(1)}, u32[]{:S(2)}, u32[]{:S(2)}) %collective-permute-start.5) | collective-permute-done | bytes 1064992 | tf_op jit(solution)/shard_map/s1/ppermute | solution.py:298
  70.0 1.8 %collective-permute-start.9 = (bf16[32,8320]{1,0:T(8,128)(2,1)S(1)}, bf16[32,8320]{1,0:T(8,128)(2,1)S(1)}, u32[]{:S(2)}, u32[]{:S(2)}) collective-permute-start(bf16[32,8320]{1,0:T(8,128)(2,1)S(1)} %get-tuple-element.49), channel_id=1, source_target_pairs={{0,64},{8,72},{16,80},{24,88},{32,96},{40,104},{48,112},{56,120},{... | collective-permute-start | bytes 1597448 | tf_op jit(solution)/shard_map/t1b/ppermute | solution.py:298
  72.1 5.4 %score_and_deal.2 = (bf16[128,1152]{1,0:T(8,128)(2,1)S(1)}, bf16[128,1152]{1,0:T(8,128)(2,1)S(1)}, bf16[128,1152]{1,0:T(8,128)(2,1)S(1)}, bf16[128,1152]{1,0:T(8,128)(2,1)S(1)}) custom-call(s32[15]{0:T(128)S(1)} %stack.55.place.which, bf16[64,8320]{1,0:T(8,128)(2,1)S(1)} %collective-permute-done.1.refs_0_, ...), custom_call_target="tpu_custom_call" | custom-call | flops 4294967296 | bytes 16777216 | tf_op jit(solution)/shard_map/score_and_deal/pallas_call | solution.py:188
  77.5 5.3 %score_group.3.refs_7_ = bf16[256,1152]{1,0:T(8,128)(2,1)S(1)} custom-call(s32[15]{0:T(128)S(1)} %stack.55.place.which, bf16[64,8320]{1,0:T(8,128)(2,1)S(1)} %collective-permute-done.refs_0_, bf16[64,8320]{1,0:T(8,128)(2,1)S(1)} %collective-permute-done.5.refs_1_, bf16[64,8320]{1,0:T(8,128)(2,1)S(1)} %collective-permute-done.14.refs_2_, ...), custom_call_target="tpu_custom_call" | custom-call | flops 4294967296 | bytes 16777216 | tf_op jit(solution)/shard_map/score_group/pallas_call | solution.py:188
  84.0 1.6 %collective-permute-done.8.refs_1_ = bf16[32,8320]{1,0:T(8,128)(2,1)S(1)} collective-permute-done((bf16[32,8320]{1,0:T(8,128)(2,1)S(1)}, bf16[32,8320]{1,0:T(8,128)(2,1)S(1)}, u32[]{:S(2)}, u32[]{:S(2)}) %collective-permute-start.8) | collective-permute-done | bytes 532512 | tf_op jit(solution)/shard_map/t1a/ppermute | solution.py:298
  87.2 1.7 %collective-permute-start.21 = (bf16[128,1152]{1,0:T(8,128)(2,1)S(1)}, bf16[128,1152]{1,0:T(8,128)(2,1)S(1)}, u32[]{:S(2)}, u32[]{:S(2)}) collective-permute-start(bf16[128,1152]{1,0:T(8,128)(2,1)S(1)} %get-tuple-element.60), channel_id=1, source_target_pairs={{0,6},{1,7},{2,0},{3,1},{4,2},{5,3},{6,4},{7,5},{8,14},{9,15},{10,... | collective-permute-start | bytes 884744 | tf_op jit(solution)/shard_map/down_oq/ppermute | solution.py:302
  88.9 1.8 %collective-permute-start.22 = (bf16[128,1152]{1,0:T(8,128)(2,1)S(1)}, bf16[128,1152]{1,0:T(8,128)(2,1)S(1)}, u32[]{:S(2)}, u32[]{:S(2)}) collective-permute-start(bf16[128,1152]{1,0:T(8,128)(2,1)S(1)} %get-tuple-element.59), channel_id=1, source_target_pairs={{0,4},{1,5},{2,6},{3,7},{4,0},{5,1},{6,2},{7,3},{8,12},{9,13},{10,... | collective-permute-start | bytes 884744 | tf_op jit(solution)/shard_map/over_oq/ppermute | solution.py:302
  90.7 5.4 %score_and_deal.3 = (bf16[128,1152]{1,0:T(8,128)(2,1)S(1)}, bf16[128,1152]{1,0:T(8,128)(2,1)S(1)}, bf16[128,1152]{1,0:T(8,128)(2,1)S(1)}, bf16[128,1152]{1,0:T(8,128)(2,1)S(1)}) custom-call(s32[15]{0:T(128)S(1)} %stack.55.place.which, bf16[64,8320]{1,0:T(8,128)(2,1)S(1)} %collective-permute-done.3.b.refs_0_, ...), custom_call_target="tpu_custom_call" | custom-call | flops 4294967296 | bytes 16777216 | tf_op jit(solution)/shard_map/score_and_deal/pallas_call | solution.py:188
  96.8 2.6 %collective-permute-start.18 = (bf16[128,1152]{1,0:T(8,128)(2,1)S(1)}, bf16[128,1152]{1,0:T(8,128)(2,1)S(1)}, u32[]{:S(2)}, u32[]{:S(2)}) collective-permute-start(bf16[128,1152]{1,0:T(8,128)(2,1)S(1)} %get-tuple-element.67), channel_id=1, source_target_pairs={{0,6},{1,7},{2,0},{3,1},{4,2},{5,3},{6,4},{7,5},{8,14},{9,15},{10,... | collective-permute-start | bytes 884744 | tf_op jit(solution)/shard_map/down_st/ppermute | solution.py:302
  101.2 2.8 %collective-permute-done.22.c = bf16[128,1152]{1,0:T(8,128)(2,1)S(1)} collective-permute-done((bf16[128,1152]{1,0:T(8,128)(2,1)S(1)}, bf16[128,1152]{1,0:T(8,128)(2,1)S(1)}, u32[]{:S(2)}, u32[]{:S(2)}) %collective-permute-start.22) | collective-permute-done | bytes 294944 | tf_op jit(solution)/shard_map/over_oq/ppermute | solution.py:302
  104.4 5.6 %collective-permute-start.24 = (bf16[128,1152]{1,0:T(8,128)(2,1)S(1)}, bf16[128,1152]{1,0:T(8,128)(2,1)S(1)}, u32[]{:S(2)}, u32[]{:S(2)}) collective-permute-start(bf16[128,1152]{1,0:T(8,128)(2,1)S(1)} %get-tuple-element.72), channel_id=1, source_target_pairs={{1,0},{2,3},{5,4},{6,7},{9,8},{10,11},{13,12},{14,15},{16,17},{19,... | collective-permute-start | bytes 884744 | tf_op jit(solution)/shard_map/oq/ppermute | solution.py:302
  110.3 6.0 %collective-permute-done.19.c = bf16[128,1152]{1,0:T(8,128)(2,1)S(1)} collective-permute-done((bf16[128,1152]{1,0:T(8,128)(2,1)S(1)}, bf16[128,1152]{1,0:T(8,128)(2,1)S(1)}, u32[]{:S(2)}, u32[]{:S(2)}) %collective-permute-start.19) | collective-permute-done | bytes 294944 | tf_op jit(solution)/shard_map/over_st/ppermute | solution.py:302
  118.0 10.7 %collective-permute-done.23.refs_2_ = bf16[128,1152]{1,0:T(8,128)(2,1)S(1)} collective-permute-done((bf16[128,1152]{1,0:T(8,128)(2,1)S(1)}, bf16[128,1152]{1,0:T(8,128)(2,1)S(1)}, u32[]{:S(2)}, u32[]{:S(2)}) %collective-permute-start.23) | collective-permute-done | bytes 294944 | tf_op jit(solution)/shard_map/st/ppermute | solution.py:302
  128.7 1.7 %finish.1 = f32[128,1024]{1,0:T(8,128)} custom-call(s32[15]{0:T(128)S(1)} %stack.55.place.which, f32[128,1152]{1,0:T(8,128)S(1)} %get-tuple-element.69.refs_0_, f32[128,1152]{1,0:T(8,128)S(1)} %get-tuple-element.70.refs_1_, bf16[128,1152]{1,0:T(8,128)(2,1)S(1)} %collective-permute-done.23.refs_2_, bf16[128,1152]{1,0:T(8,128)(2,1)S(1)} %collective-permute-done.24.refs_3_), custom_call_target="tpu_custom_call" | custom-call | tf_op jit(solution)/shard_map/finish/pallas_call | solution.py:249
  (43 shorter events, 13.3 us)
Async XLA Ops:
  12.9 25.3 %collective-permute-start = (bf16[64,8320]{1,0:T(8,128)(2,1)S(1)}, bf16[64,8320]{1,0:T(8,128)(2,1)S(1)}, u32[]{:S(2)}, u32[]{:S(2)}) collective-permute-start(bf16[64,8320]{1,0:T(8,128)(2,1)S(1)} %condition.1.refs_0_), channel_id=1, source_target_pairs={{0,16},{8,24},{16,0},{24,8},{32,48},{40,56},{48,32},{56,40},{64,80... | collective-permute-start | bytes 3194888 | tf_op jit(solution)/shard_map/s0/ppermute | solution.py:298
  13.3 25.7 %collective-permute-start.1 = (bf16[64,8320]{1,0:T(8,128)(2,1)S(1)}, bf16[64,8320]{1,0:T(8,128)(2,1)S(1)}, u32[]{:S(2)}, u32[]{:S(2)}) collective-permute-start(bf16[64,8320]{1,0:T(8,128)(2,1)S(1)} %condition.1.refs_0_), channel_id=1, source_target_pairs={{0,48},{8,56},{16,32},{24,40},{32,16},{40,24},{48,0},{56,8},{64,11... | collective-permute-start | bytes 3194888 | tf_op jit(solution)/shard_map/q0/ppermute | solution.py:298
  15.8 24.9 %collective-permute-start.2 = (bf16[64,8320]{1,0:T(8,128)(2,1)S(1)}, bf16[64,8320]{1,0:T(8,128)(2,1)S(1)}, u32[]{:S(2)}, u32[]{:S(2)}) collective-permute-start(bf16[64,8320]{1,0:T(8,128)(2,1)S(1)} %condition.1.refs_0_), channel_id=1, source_target_pairs={{0,64},{8,72},{16,80},{24,88},{32,96},{40,104},{48,112},{56,120},{... | collective-permute-start | bytes 3194888 | tf_op jit(solution)/shard_map/o1/ppermute | solution.py:298
  17.7 27.5 %collective-permute-start.6 = (bf16[64,8320]{1,0:T(8,128)(2,1)S(1)}, bf16[64,8320]{1,0:T(8,128)(2,1)S(1)}, u32[]{:S(2)}, u32[]{:S(2)}) collective-permute-start(bf16[64,8320]{1,0:T(8,128)(2,1)S(1)} %condition.1.refs_0_), channel_id=1, source_target_pairs={{0,8},{8,0},{16,24},{24,16},{32,40},{40,32},{48,56},{56,48},{64,72... | collective-permute-start | bytes 3194888 | tf_op jit(solution)/shard_map/own_sib/ppermute | solution.py:298
  40.6 4.6 %collective-permute-start.7 = (bf16[64,8320]{1,0:T(8,128)(2,1)S(1)}, bf16[64,8320]{1,0:T(8,128)(2,1)S(1)}, u32[]{:S(2)}, u32[]{:S(2)}) collective-permute-start(bf16[64,8320]{1,0:T(8,128)(2,1)S(1)} %collective-permute-done.2.refs_1_), channel_id=1, source_target_pairs={{0,8},{8,0},{16,24},{24,16},{32,40},{40,32},{48,56},{56,48},{64,72... | collective-permute-start | bytes 3194888 | tf_op jit(solution)/shard_map/o1_sib/ppermute | solution.py:298
  40.6 26.6 %collective-permute-start.4 = (bf16[64,8320]{1,0:T(8,128)(2,1)S(1)}, bf16[64,8320]{1,0:T(8,128)(2,1)S(1)}, u32[]{:S(2)}, u32[]{:S(2)}) collective-permute-start(bf16[64,8320]{1,0:T(8,128)(2,1)S(1)} %collective-permute-done.2.refs_1_), channel_id=1, source_target_pairs={{0,48},{8,56},{16,32},{24,40},{32,16},{40,24},{48,0},{56,8},{64,11... | collective-permute-start | bytes 3194888 | tf_op jit(solution)/shard_map/q1/ppermute | solution.py:298
  40.9 26.3 %collective-permute-start.3 = (bf16[64,8320]{1,0:T(8,128)(2,1)S(1)}, bf16[64,8320]{1,0:T(8,128)(2,1)S(1)}, u32[]{:S(2)}, u32[]{:S(2)}) collective-permute-start(bf16[64,8320]{1,0:T(8,128)(2,1)S(1)} %collective-permute-done.1.refs_0_), channel_id=1, source_target_pairs={{0,16},{8,24},{16,0},{24,8},{32,48},{40,56},{48,32},{56,40},{64,80... | collective-permute-start | bytes 3194888 | tf_op jit(solution)/shard_map/t0/ppermute | solution.py:298
  43.3 25.5 %collective-permute-start.5 = (bf16[64,8320]{1,0:T(8,128)(2,1)S(1)}, bf16[64,8320]{1,0:T(8,128)(2,1)S(1)}, u32[]{:S(2)}, u32[]{:S(2)}) collective-permute-start(bf16[64,8320]{1,0:T(8,128)(2,1)S(1)} %collective-permute-done.refs_0_), channel_id=1, source_target_pairs={{0,64},{8,72},{16,80},{24,88},{32,96},{40,104},{48,112},{56,120},{... | collective-permute-start | bytes 3194888 | tf_op jit(solution)/shard_map/s1/ppermute | solution.py:298
  45.2 24.7 %collective-permute-start.10 = (bf16[64,8320]{1,0:T(8,128)(2,1)S(1)}, bf16[64,8320]{1,0:T(8,128)(2,1)S(1)}, u32[]{:S(2)}, u32[]{:S(2)}) collective-permute-start(bf16[64,8320]{1,0:T(8,128)(2,1)S(1)} %collective-permute-done.1.refs_0_), channel_id=1, source_target_pairs={{0,8},{8,0},{16,24},{24,16},{32,40},{40,32},{48,56},{56,48},{64,72... | collective-permute-start | bytes 3194888 | tf_op jit(solution)/shard_map/q0_sib/ppermute | solution.py:298
  68.9 8.6 %collective-permute-start.12 = (bf16[64,8320]{1,0:T(8,128)(2,1)S(1)}, bf16[64,8320]{1,0:T(8,128)(2,1)S(1)}, u32[]{:S(2)}, u32[]{:S(2)}) collective-permute-start(bf16[64,8320]{1,0:T(8,128)(2,1)S(1)} %collective-permute-done.5.refs_1_), channel_id=1, source_target_pairs={{0,8},{8,0},{16,24},{24,16},{32,40},{40,32},{48,56},{56,48},{64,72... | collective-permute-start | bytes 3194888 | tf_op jit(solution)/shard_map/s1_sib/ppermute | solution.py:298
  69.4 8.1 %collective-permute-start.13 = (bf16[64,8320]{1,0:T(8,128)(2,1)S(1)}, bf16[64,8320]{1,0:T(8,128)(2,1)S(1)}, u32[]{:S(2)}, u32[]{:S(2)}) collective-permute-start(bf16[64,8320]{1,0:T(8,128)(2,1)S(1)} %collective-permute-done.3.b.refs_0_), channel_id=1, source_target_pairs={{0,8},{8,0},{16,24},{24,16},{32,40},{40,32},{48,56},{56,48},{64,72... | collective-permute-start | bytes 3194888 | tf_op jit(solution)/shard_map/t0_sib/ppermute | solution.py:298
  69.4 8.1 %collective-permute-start.14 = (bf16[64,8320]{1,0:T(8,128)(2,1)S(1)}, bf16[64,8320]{1,0:T(8,128)(2,1)S(1)}, u32[]{:S(2)}, u32[]{:S(2)}) collective-permute-start(bf16[64,8320]{1,0:T(8,128)(2,1)S(1)} %collective-permute-done.refs_0_), channel_id=1, source_target_pairs={{0,8},{8,0},{16,24},{24,16},{32,40},{40,32},{48,56},{56,48},{64,72... | collective-permute-start | bytes 3194888 | tf_op jit(solution)/shard_map/s0_sib/ppermute | solution.py:298
  70.0 14.1 %collective-permute-start.9 = (bf16[32,8320]{1,0:T(8,128)(2,1)S(1)}, bf16[32,8320]{1,0:T(8,128)(2,1)S(1)}, u32[]{:S(2)}, u32[]{:S(2)}) collective-permute-start(bf16[32,8320]{1,0:T(8,128)(2,1)S(1)} %get-tuple-element.49), channel_id=1, source_target_pairs={{0,64},{8,72},{16,80},{24,88},{32,96},{40,104},{48,112},{56,120},{... | collective-permute-start | bytes 1597448 | tf_op jit(solution)/shard_map/t1b/ppermute | solution.py:298
  71.8 13.9 %collective-permute-start.8 = (bf16[32,8320]{1,0:T(8,128)(2,1)S(1)}, bf16[32,8320]{1,0:T(8,128)(2,1)S(1)}, u32[]{:S(2)}, u32[]{:S(2)}) collective-permute-start(bf16[32,8320]{1,0:T(8,128)(2,1)S(1)} %get-tuple-element.48), channel_id=1, source_target_pairs={{0,16},{8,24},{16,0},{24,8},{32,48},{40,56},{48,32},{56,40},{64,80... | collective-permute-start | bytes 1597448 | tf_op jit(solution)/shard_map/t1a/ppermute | solution.py:298
  84.0 6.7 %collective-permute-start.16 = (bf16[32,8320]{1,0:T(8,128)(2,1)S(1)}, bf16[32,8320]{1,0:T(8,128)(2,1)S(1)}, u32[]{:S(2)}, u32[]{:S(2)}) collective-permute-start(bf16[32,8320]{1,0:T(8,128)(2,1)S(1)} %collective-permute-done.9.refs_2_), channel_id=1, source_target_pairs={{0,8},{8,0},{16,24},{24,16},{32,40},{40,32},{48,56},{56,48},{64,72... | collective-permute-start | bytes 1597448 | tf_op jit(solution)/shard_map/t1_sib/ppermute | solution.py:298
  85.7 5.1 %collective-permute-start.15 = (bf16[32,8320]{1,0:T(8,128)(2,1)S(1)}, bf16[32,8320]{1,0:T(8,128)(2,1)S(1)}, u32[]{:S(2)}, u32[]{:S(2)}) collective-permute-start(bf16[32,8320]{1,0:T(8,128)(2,1)S(1)} %collective-permute-done.8.refs_1_), channel_id=1, source_target_pairs={{0,8},{8,0},{16,24},{24,16},{32,40},{40,32},{48,56},{56,48},{64,72... | collective-permute-start | bytes 1597448 | tf_op jit(solution)/shard_map/t1_sib/ppermute | solution.py:298
  85.7 13.8 %collective-permute-start.20 = (bf16[128,1152]{1,0:T(8,128)(2,1)S(1)}, bf16[128,1152]{1,0:T(8,128)(2,1)S(1)}, u32[]{:S(2)}, u32[]{:S(2)}) collective-permute-start(bf16[128,1152]{1,0:T(8,128)(2,1)S(1)} %get-tuple-element.58), channel_id=1, source_target_pairs={{0,2},{1,3},{2,4},{3,5},{4,6},{5,7},{6,0},{7,1},{8,10},{9,11},{10,... | collective-permute-start | bytes 884744 | tf_op jit(solution)/shard_map/up_oq/ppermute | solution.py:302
  87.2 14.1 %collective-permute-start.21 = (bf16[128,1152]{1,0:T(8,128)(2,1)S(1)}, bf16[128,1152]{1,0:T(8,128)(2,1)S(1)}, u32[]{:S(2)}, u32[]{:S(2)}) collective-permute-start(bf16[128,1152]{1,0:T(8,128)(2,1)S(1)} %get-tuple-element.60), channel_id=1, source_target_pairs={{0,6},{1,7},{2,0},{3,1},{4,2},{5,3},{6,4},{7,5},{8,14},{9,15},{10,... | collective-permute-start | bytes 884744 | tf_op jit(solution)/shard_map/down_oq/ppermute | solution.py:302
  88.9 15.1 %collective-permute-start.22 = (bf16[128,1152]{1,0:T(8,128)(2,1)S(1)}, bf16[128,1152]{1,0:T(8,128)(2,1)S(1)}, u32[]{:S(2)}, u32[]{:S(2)}) collective-permute-start(bf16[128,1152]{1,0:T(8,128)(2,1)S(1)} %get-tuple-element.59), channel_id=1, source_target_pairs={{0,4},{1,5},{2,6},{3,7},{4,0},{5,1},{6,2},{7,3},{8,12},{9,13},{10,... | collective-permute-start | bytes 884744 | tf_op jit(solution)/shard_map/over_oq/ppermute | solution.py:302
  96.2 14.1 %collective-permute-start.17 = (bf16[128,1152]{1,0:T(8,128)(2,1)S(1)}, bf16[128,1152]{1,0:T(8,128)(2,1)S(1)}, u32[]{:S(2)}, u32[]{:S(2)}) collective-permute-start(bf16[128,1152]{1,0:T(8,128)(2,1)S(1)} %get-tuple-element.66), channel_id=1, source_target_pairs={{0,2},{1,3},{2,4},{3,5},{4,6},{5,7},{6,0},{7,1},{8,10},{9,11},{10,... | collective-permute-start | bytes 884744 | tf_op jit(solution)/shard_map/up_st/ppermute | solution.py:302
  96.8 13.4 %collective-permute-start.18 = (bf16[128,1152]{1,0:T(8,128)(2,1)S(1)}, bf16[128,1152]{1,0:T(8,128)(2,1)S(1)}, u32[]{:S(2)}, u32[]{:S(2)}) collective-permute-start(bf16[128,1152]{1,0:T(8,128)(2,1)S(1)} %get-tuple-element.67), channel_id=1, source_target_pairs={{0,6},{1,7},{2,0},{3,1},{4,2},{5,3},{6,4},{7,5},{8,14},{9,15},{10,... | collective-permute-start | bytes 884744 | tf_op jit(solution)/shard_map/down_st/ppermute | solution.py:302
  99.5 16.8 %collective-permute-start.19 = (bf16[128,1152]{1,0:T(8,128)(2,1)S(1)}, bf16[128,1152]{1,0:T(8,128)(2,1)S(1)}, u32[]{:S(2)}, u32[]{:S(2)}) collective-permute-start(bf16[128,1152]{1,0:T(8,128)(2,1)S(1)} %get-tuple-element.68), channel_id=1, source_target_pairs={{0,4},{1,5},{2,6},{3,7},{4,0},{5,1},{6,2},{7,3},{8,12},{9,13},{10,... | collective-permute-start | bytes 884744 | tf_op jit(solution)/shard_map/over_st/ppermute | solution.py:302
  104.4 13.6 %collective-permute-start.24 = (bf16[128,1152]{1,0:T(8,128)(2,1)S(1)}, bf16[128,1152]{1,0:T(8,128)(2,1)S(1)}, u32[]{:S(2)}, u32[]{:S(2)}) collective-permute-start(bf16[128,1152]{1,0:T(8,128)(2,1)S(1)} %get-tuple-element.72), channel_id=1, source_target_pairs={{1,0},{2,3},{5,4},{6,7},{9,8},{10,11},{13,12},{14,15},{16,17},{19,... | collective-permute-start | bytes 884744 | tf_op jit(solution)/shard_map/oq/ppermute | solution.py:302
  116.7 12.0 %collective-permute-start.23 = (bf16[128,1152]{1,0:T(8,128)(2,1)S(1)}, bf16[128,1152]{1,0:T(8,128)(2,1)S(1)}, u32[]{:S(2)}, u32[]{:S(2)}) collective-permute-start(bf16[128,1152]{1,0:T(8,128)(2,1)S(1)} %get-tuple-element.71), channel_id=1, source_target_pairs={{0,1},{3,2},{4,5},{7,6},{8,9},{11,10},{12,13},{15,14},{17,16},{18,... | collective-permute-start | bytes 884744 | tf_op jit(solution)/shard_map/st/ppermute | solution.py:302
  (4 other events, 5.8 us)
where the time goes:
time: 131 us
  waiting for transfers between devices  50.4 us (38%)
  Pallas kernels  33.9 us (26%)
  starting transfers between devices  28.3 us (22%)
  local copies, waits for them, and re-layouts  17.7 us (14%)
    ppermute x17, waiting for transfers between devices, send(): return lax.ppermute(value, 'rows', pairs)  29.4 us
    pallas_call x4, Pallas kernels, score_group(): pl.pallas_call(kernel, out_shape=out, in_specs=[pl.BlockSpec(memory_space...  21.4 us
    ppermute x8, waiting for transfers between devices, whole(): return lax.ppermute(value, BOTH, whole_perm(move))  21 us
    unnamed x7, local copies, waits for them, and re-layouts  17.6 us
    ppermute x8, starting transfers between devices, whole(): return lax.ppermute(value, BOTH, whole_perm(move))  15.8 us
    ppermute x17, starting transfers between devices, send(): return lax.ppermute(value, 'rows', pairs)  12.5 us
    pallas_call x1, Pallas kernels, condition(): pl.pallas_call(condition_kernel, out_shape=jax.ShapeDtypeStruct((count, l...  9.9 us
  transfers between devices with their start and end apart: 25, of which 12 were waited for; matrix products, arithmetic and copies ran while one was open for 11% of the time, Pallas kernels for 17%

commit v1 on v0

--- a/solution.py
+++ b/solution.py
@@ -71,7 +71,7 @@
     return lax.dot_general(a, b, (((1,), (0,)), ((), ())), preferred_element_type=F32)
 
 def condition_kernel(q, left, right, out, swapped, back, turned_left):
-    count, layers, width = q.shape
+    layers, count, width = q.shape
     side = right.shape[1]
     four = 4 * side
     tiles = width // 128
@@ -83,7 +83,7 @@
     for l in range(layers):
         lanes = jnp.concatenate([right[l]] * 4, axis=1)
         wide_r = jnp.where(right_mask, jnp.concatenate([lanes] * 4, axis=0), 0.0)
-        x = q[:, l, :]
+        x = q[l]
         rows = jnp.concatenate([x[:, four * g : four * (g + 1)] for g in range(width // four)], axis=0)
         first = sum(dot(rows, part) for part in reversed(thirds(wide_r)))
         for g in range(width // four):
@@ -121,19 +121,24 @@
             total = total + wide * wide
     out[:, layers * width :] = norm_columns(jnp.sum(total, axis=1, keepdims=True))
 
-def condition(q, left, right, first, count):
-    _, layers, width = q.shape
+def condition(q, left, right):
+    layers, count, width = q.shape
+    side = left.shape[1]
+    vmem = pl.BlockSpec(memory_space=pltpu.VMEM)
     return pl.pallas_call(
         condition_kernel,
         out_shape=jax.ShapeDtypeStruct((count, layers * width + PAD), BF),
-        grid=(1,),
-        in_specs=[pl.BlockSpec((count, layers, width), lambda i: (first, 0, 0)),
-            pl.BlockSpec(left.shape, lambda i: (0, 0, 0)), pl.BlockSpec(right.shape, lambda i: (0, 0, 0))],
-        out_specs=pl.BlockSpec((count, layers * width + PAD), lambda i: (0, 0)),
-        scratch_shapes=[pltpu.VMEM((width // 128, count, 128), F32), pltpu.VMEM((count, width // 128, 128), F32), pltpu.VMEM((3, left.shape[1], 128), F32)],
+        in_specs=[vmem] * 3,
+        out_specs=vmem,
+        scratch_shapes=[
+            pltpu.VMEM((width // 128, count, 128), F32),
+            pltpu.VMEM((count, width // 128, 128), F32),
+            pltpu.VMEM((3, side, 128), F32),
+        ],
         compiler_params=pltpu.CompilerParams(vmem_limit_bytes=24 * MIB),
         name="condition",
     )(q, left, right)
+
 
 def fill(at, place, pieces, group):
     for i, piece in enumerate(pieces):
@@ -222,40 +227,28 @@
     )(*blocks)
 
 
-def finish_kernel(at, which, *refs):
-    *blocks, out, keep, got, sems = refs
-    kinds = len(blocks) // 2
+def finish_kernel(at, which, keep_0, keep_1, got_0, got_1, out):
     edge = out.shape[1]
-    for i in range(kinds):
-
-        @pl.when(which[at] == i)
-        def _(i=i):
-            one = pltpu.make_async_copy(blocks[i], keep, sems.at[0])
-            two = pltpu.make_async_copy(blocks[kinds + i], got, sems.at[1])
-            one.start()
-            two.start()
-            one.wait()
-            two.wait()
-
-    more = got[...].astype(F32)
-    norms = keep[:, edge : edge + 1] + (
-        more[:, edge : edge + 1] + more[:, edge + PAD // 2 : edge + PAD // 2 + 1]
-    )
-    out[...] = (keep[:, :edge] + more[:, :edge]) * lax.rsqrt(norms + EPS)
+
+    def write(keep, got):
+        more = got[...].astype(F32)
+        norms = keep[:, edge : edge + 1] + (
+            more[:, edge : edge + 1] + more[:, edge + PAD // 2 : edge + PAD // 2 + 1]
+        )
+        out[...] = (keep[:, :edge] + more[:, :edge]) * lax.rsqrt(norms + EPS)
+
+    pl.when(which[at] == 0)(lambda: write(keep_0, got_0))
+    pl.when(which[at] != 0)(lambda: write(keep_1, got_1))
 
 
 def finish(which, at, keeps, gots):
     rows, width = keeps[0].shape
+    vmem = pl.BlockSpec(memory_space=pltpu.VMEM)
     return pl.pallas_call(
         functools.partial(finish_kernel, at),
         out_shape=jax.ShapeDtypeStruct((rows, width - PAD), F32),
-        in_specs=[pl.BlockSpec(memory_space=pltpu.SMEM)]
-        + [pl.BlockSpec(memory_space=pl.ANY)] * (2 * len(keeps)),
-        scratch_shapes=[
-            pltpu.VMEM((rows, width), F32),
-            pltpu.VMEM((rows, width), BF),
-            pltpu.SemaphoreType.DMA((2,)),
-        ],
+        in_specs=[pl.BlockSpec(memory_space=pltpu.SMEM)] + [vmem] * 4,
+        out_specs=vmem,
         compiler_params=pltpu.CompilerParams(vmem_limit_bytes=4 * MIB),
         name="finish",
     )(which, *keeps, *gots)
@@ -322,16 +315,16 @@
             whole(down, lambda zz, yy, xx, hh: (xx - 1, hh), "down" + name),
             whole(over, lambda zz, yy, xx, hh: (xx + 2, hh), "over" + name),
         ]
-        return sum_blocks([mine, *got])
+        return mine, *got
 
     one = ((n,), (n,))
     cut = n // 2
-    tables = [place(one), place(((n,), (cut, cut))), dealt(), [(x % 2 == side) == (zh == y % 2)]]
+    tables = [place(one), dealt(), place(((n,), (cut, cut))), [(x % 2 == side) == (zh == y % 2)]]
     starts = [sum(len(t) for t in tables[:i]) for i in range(len(tables))]
     table = jnp.stack([jnp.asarray(v, jnp.int32) for t in tables for v in t])
     queries, table = lax.optimization_barrier((queries, table))
 
-    own = condition(queries, left_inverse, right_inverse, 0, n)
+    own = condition(jnp.swapaxes(queries, 0, 1), left_inverse, right_inverse)
     s0 = send(own, SAME, "s0")
     q0 = send(own, OPPOSITE, "q0")
     o1 = send(own, ACROSS, "o1")
@@ -344,19 +337,20 @@
     o1_sib, q0_sib, s0_sib = send(o1, SIBLING, "o1_sib"), send(q0, SIBLING, "q0_sib"), send(s0, SIBLING, "s0_sib")
     scores_o = score_group(table, starts[0], [own, o1, own_sib, o1_sib], stored)
 
-    t0, q1, s1, scores_o = lax.optimization_barrier((t0, q1, s1, scores_o))
+    t0, q1, s1, scores_o, s0_sib = lax.optimization_barrier((t0, q1, s1, scores_o, s0_sib))
     first, second = split(q1, t0, cut)
-    last = [send(first, SAME, "t1a"), send(second, ACROSS, "t1b")]
+    t1a, t1b = send(first, SAME, "t1a"), send(second, ACROSS, "t1b")
     q1_sib, s1_sib, t0_sib = send(q1, SIBLING, "q1_sib"), send(s1, SIBLING, "s1_sib"), send(t0, SIBLING, "t0_sib")
-    dealt_1 = score_group(table, starts[0], [q0, q1, q0_sib, q1_sib], stored, scores_o, starts[2])
+    dealt_1 = score_group(table, starts[0], [q0, q1, q0_sib, q1_sib], stored, scores_o, starts[1])
     *dealt_1, s1_sib, t0_sib = lax.optimization_barrier((*dealt_1, s1_sib, t0_sib))
+    mine, up, down, over = reduce_batch(dealt_1, "_oq")
     scores_s = score_group(table, starts[0], [after(s0, *dealt_1), s1, s0_sib, s1_sib], stored)
-    last_sib = [send(after(piece, scores_s), SIBLING, "t1_sib") for piece in last]
-    keep_1, onward_1 = reduce_batch(dealt_1, "_oq")
-    dealt_2 = score_group(
-        table, starts[1], [t0, *last, t0_sib, *last_sib], stored, scores_s, starts[2]
-    )
-    keep_2, onward_2 = reduce_batch(dealt_2, "_st")
+    t1a, t1b, scores_s, up, down = lax.optimization_barrier((t1a, t1b, scores_s, up, down))
+    t1a_sib, t1b_sib = send(t1a, SIBLING, "t1a_sib"), send(t1b, SIBLING, "t1b_sib")
+    keep_1, onward_1 = sum_blocks([mine, up, down, over])
+    last = [t0, t1a, t1b, t0_sib, t1a_sib, t1b_sib]
+    dealt_2 = score_group(table, starts[2], last, stored, scores_s, starts[1])
+    keep_2, onward_2 = sum_blocks(reduce_batch(dealt_2, "_st"))
 
     def final_first(yy, xx, hh):
         return (xx % 2 == yy // 2) == (hh == yy % 2)

time: 131 us -> 125 us (0.954)
  waiting for transfers between devices: 50.4 us -> 45 us
  Pallas kernels: 33.9 us -> 31.6 us
  starting transfers between devices: 28.3 us -> 30.4 us
    ppermute x17, waiting for transfers between devices: 29.4 us -> 26.1 us  [send(): return lax.ppermute(value, 'rows', pairs)]
    unnamed x7 -> x5, local copies, waits for them, and re-layouts: 17.6 us -> 14.7 us
    ppermute x8, waiting for transfers between devices: 21 us -> 18.9 us  [whole(): return lax.ppermute(value, BOTH, whole_perm(move))]
    pallas_call x1, Pallas kernels: 9.9 us -> 7.84 us  [condition(): pl.pallas_call(condition_kernel, out_shape=jax.ShapeDtypeStruct((count, l...]
    optimization_barrier x0 -> x1, local copies, waits for them, and re-layouts: none -> 1.81 us  [per_device(): queries, table = lax.optimization_barrier((queries, table))]
    ppermute x8, starting transfers between devices: 15.8 us -> 17.2 us  [whole(): return lax.ppermute(value, BOTH, whole_perm(move))]
  transfers between devices with their start and end apart: 25 -> 25, of which waited for: 12 -> 9; matrix products, arithmetic and copies ran while one was open for 11% -> 12% of each run, Pallas kernels for 17% -> 18%
where the time goes in v1:
time: 125 us; the launch traced here: 124 us
  waiting for transfers between devices  45 us (36%)
  Pallas kernels  31.6 us (25%)
  starting transfers between devices  30.4 us (24%)
  local copies, waits for them, and re-layouts  16.6 us (13%)
    ppermute x17, waiting for transfers between devices, send(): return lax.ppermute(value, 'rows', pairs)  26.1 us
    pallas_call x4, Pallas kernels, score_group(): pl.pallas_call(kernel, out_shape=out, in_specs=[pl.BlockSpec(memory_space...  21.4 us
    ppermute x8, waiting for transfers between devices, whole(): return lax.ppermute(value, BOTH, whole_perm(move))  18.9 us
    ppermute x8, starting transfers between devices, whole(): return lax.ppermute(value, BOTH, whole_perm(move))  17.2 us
    unnamed x5, local copies, waits for them, and re-layouts  14.7 us
    ppermute x17, starting transfers between devices, send(): return lax.ppermute(value, 'rows', pairs)  13.2 us
    pallas_call x1, Pallas kernels, condition(): pl.pallas_call(condition_kernel, out_shape=jax.ShapeDtypeStruct((count, l...  7.84 us
  transfers between devices with their start and end apart: 25, of which 9 were waited for; matrix products, arithmetic and copies ran while one was open for 12% of the time, Pallas kernels for 18%

profile of v1, /device:TPU:8, one launch (start us, length us, event | category | flops | bytes accessed | tf_op | source)
XLA Modules:
  0.0 123.8 jit_solution(3696574262107101850)
XLA Ops:
  0.1 1.8 %copy.8 = bf16[64,2,4096]{2,0,1:T(8,128)(2,1)S(1)} copy(bf16[64,2,4096]{2,1,0:T(2,128)(2,1)} %param.4) | data formatting | bytes 2097152 | tf_op jit(solution)/shard_map/optimization_barrier | solution.py:325
  1.9 7.8 %condition.1.refs_0_ = bf16[64,8320]{1,0:T(8,128)(2,1)S(1)} custom-call(bf16[2,64,4096]{2,1,0:T(8,128)(2,1)S(1)} %bitcast.20, f32[2,64,64]{2,1,0:T(8,128)S(1)} %copy-done, f32[2,64,64]{2,1,0:T(8,128)S(1)} %copy-done.1), custom_call_target="tpu_custom_call" | custom-call | tf_op jit(solution)/shard_map/condition/pallas_call | solution.py:128
  10.2 2.5 %collective-permute-start.1 = (bf16[64,8320]{1,0:T(8,128)(2,1)S(1)}, bf16[64,8320]{1,0:T(8,128)(2,1)S(1)}, u32[]{:S(2)}, u32[]{:S(2)}) collective-permute-start(bf16[64,8320]{1,0:T(8,128)(2,1)S(1)} %condition.1.refs_0_), channel_id=1, source_target_pairs={{0,48},{8,56},{16,32},{24,40},{32,16},{40,24},{48,0},{56,8},{64,11... | collective-permute-start | bytes 3194888 | tf_op jit(solution)/shard_map/q0/ppermute | solution.py:291
  12.6 1.9 %collective-permute-start.2 = (bf16[64,8320]{1,0:T(8,128)(2,1)S(1)}, bf16[64,8320]{1,0:T(8,128)(2,1)S(1)}, u32[]{:S(2)}, u32[]{:S(2)}) collective-permute-start(bf16[64,8320]{1,0:T(8,128)(2,1)S(1)} %condition.1.refs_0_), channel_id=1, source_target_pairs={{0,64},{8,72},{16,80},{24,88},{32,96},{40,104},{48,112},{56,120},{... | collective-permute-start | bytes 3194888 | tf_op jit(solution)/shard_map/o1/ppermute | solution.py:291
  14.6 14.7 %copy.6 = bf16[128,8,2,4096]{3,1,2,0:T(8,128)(2,1)S(1)} copy(bf16[128,8,2,4096]{3,2,1,0:T(2,128)(2,1)} %bitcast.21) | data formatting | bytes 33554432
  29.3 5.8 %collective-permute-done.refs_0_ = bf16[64,8320]{1,0:T(8,128)(2,1)S(1)} collective-permute-done((bf16[64,8320]{1,0:T(8,128)(2,1)S(1)}, bf16[64,8320]{1,0:T(8,128)(2,1)S(1)}, u32[]{:S(2)}, u32[]{:S(2)}) %collective-permute-start) | collective-permute-done | bytes 1064992 | tf_op jit(solution)/shard_map/s0/ppermute | solution.py:291
  35.9 1.6 %collective-permute-done.2.refs_1_ = bf16[64,8320]{1,0:T(8,128)(2,1)S(1)} collective-permute-done((bf16[64,8320]{1,0:T(8,128)(2,1)S(1)}, bf16[64,8320]{1,0:T(8,128)(2,1)S(1)}, u32[]{:S(2)}, u32[]{:S(2)}) %collective-permute-start.2) | collective-permute-done | bytes 1064992 | tf_op jit(solution)/shard_map/o1/ppermute | solution.py:291
  37.8 2.4 %collective-permute-start.3 = (bf16[64,8320]{1,0:T(8,128)(2,1)S(1)}, bf16[64,8320]{1,0:T(8,128)(2,1)S(1)}, u32[]{:S(2)}, u32[]{:S(2)}) collective-permute-start(bf16[64,8320]{1,0:T(8,128)(2,1)S(1)} %collective-permute-done.1.refs_0_), channel_id=1, source_target_pairs={{0,16},{8,24},{16,0},{24,8},{32,48},{40,56},{48,32},{56,40},{64,80... | collective-permute-start | bytes 3194888 | tf_op jit(solution)/shard_map/t0/ppermute | solution.py:291
  40.2 1.9 %collective-permute-start.5 = (bf16[64,8320]{1,0:T(8,128)(2,1)S(1)}, bf16[64,8320]{1,0:T(8,128)(2,1)S(1)}, u32[]{:S(2)}, u32[]{:S(2)}) collective-permute-start(bf16[64,8320]{1,0:T(8,128)(2,1)S(1)} %collective-permute-done.refs_0_), channel_id=1, source_target_pairs={{0,64},{8,72},{16,80},{24,88},{32,96},{40,104},{48,112},{56,120},{... | collective-permute-start | bytes 3194888 | tf_op jit(solution)/shard_map/s1/ppermute | solution.py:291
  42.6 5.3 %score_group.2.refs_5_ = bf16[256,1152]{1,0:T(8,128)(2,1)S(1)} custom-call(s32[15]{0:T(128)S(1)} %stack.55.place.which, bf16[64,8320]{1,0:T(8,128)(2,1)S(1)} %condition.1.refs_0_, bf16[64,8320]{1,0:T(8,128)(2,1)S(1)} %collective-permute-done.2.refs_1_, bf16[64,8320]{1,0:T(8,128)(2,1)S(1)} %collective-permute-done.6.refs_2_, ...), custom_call_target="tpu_custom_call" | custom-call | flops 4294967296 | bytes 16777216 | tf_op jit(solution)/shard_map/score_group/pallas_call | solution.py:193
  47.9 16.2 %collective-permute-done.3.b.refs_0_ = bf16[64,8320]{1,0:T(8,128)(2,1)S(1)} collective-permute-done((bf16[64,8320]{1,0:T(8,128)(2,1)S(1)}, bf16[64,8320]{1,0:T(8,128)(2,1)S(1)}, u32[]{:S(2)}, u32[]{:S(2)}) %collective-permute-start.3) | collective-permute-done | bytes 1064992 | tf_op jit(solution)/shard_map/t0/ppermute | solution.py:291
  64.1 1.6 %collective-permute-done.5.refs_1_ = bf16[64,8320]{1,0:T(8,128)(2,1)S(1)} collective-permute-done((bf16[64,8320]{1,0:T(8,128)(2,1)S(1)}, bf16[64,8320]{1,0:T(8,128)(2,1)S(1)}, u32[]{:S(2)}, u32[]{:S(2)}) %collective-permute-start.5) | collective-permute-done | bytes 1064992 | tf_op jit(solution)/shard_map/s1/ppermute | solution.py:291
  66.3 1.8 %collective-permute-start.10 = (bf16[32,8320]{1,0:T(8,128)(2,1)S(1)}, bf16[32,8320]{1,0:T(8,128)(2,1)S(1)}, u32[]{:S(2)}, u32[]{:S(2)}) collective-permute-start(bf16[32,8320]{1,0:T(8,128)(2,1)S(1)} %get-tuple-element.53), channel_id=1, source_target_pairs={{0,64},{8,72},{16,80},{24,88},{32,96},{40,104},{48,112},{56,120},{... | collective-permute-start | bytes 1597448 | tf_op jit(solution)/shard_map/t1b/ppermute | solution.py:291
  68.6 5.4 %score_and_deal.2 = (bf16[128,1152]{1,0:T(8,128)(2,1)S(1)}, bf16[128,1152]{1,0:T(8,128)(2,1)S(1)}, bf16[128,1152]{1,0:T(8,128)(2,1)S(1)}, bf16[128,1152]{1,0:T(8,128)(2,1)S(1)}) custom-call(s32[15]{0:T(128)S(1)} %stack.55.place.which, bf16[64,8320]{1,0:T(8,128)(2,1)S(1)} %collective-permute-done.1.refs_0_, ...), custom_call_target="tpu_custom_call" | custom-call | flops 4294967296 | bytes 16777216 | tf_op jit(solution)/shard_map/score_and_deal/pallas_call | solution.py:193
  74.0 1.6 %collective-permute-start.15 = (bf16[128,1152]{1,0:T(8,128)(2,1)S(1)}, bf16[128,1152]{1,0:T(8,128)(2,1)S(1)}, u32[]{:S(2)}, u32[]{:S(2)}) collective-permute-start(bf16[128,1152]{1,0:T(8,128)(2,1)S(1)} %get-tuple-element.61), channel_id=1, source_target_pairs={{0,2},{1,3},{2,4},{3,5},{4,6},{5,7},{6,0},{7,1},{8,10},{9,11},{10,... | collective-permute-start | bytes 884744 | tf_op jit(solution)/shard_map/up_oq/ppermute | solution.py:295
  75.6 1.7 %collective-permute-start.16 = (bf16[128,1152]{1,0:T(8,128)(2,1)S(1)}, bf16[128,1152]{1,0:T(8,128)(2,1)S(1)}, u32[]{:S(2)}, u32[]{:S(2)}) collective-permute-start(bf16[128,1152]{1,0:T(8,128)(2,1)S(1)} %get-tuple-element.63), channel_id=1, source_target_pairs={{0,6},{1,7},{2,0},{3,1},{4,2},{5,3},{6,4},{7,5},{8,14},{9,15},{10,... | collective-permute-start | bytes 884744 | tf_op jit(solution)/shard_map/down_oq/ppermute | solution.py:295
  77.3 5.3 %score_group.3.refs_7_ = bf16[256,1152]{1,0:T(8,128)(2,1)S(1)} custom-call(s32[15]{0:T(128)S(1)} %stack.55.place.which, bf16[64,8320]{1,0:T(8,128)(2,1)S(1)} %collective-permute-done.refs_0_, bf16[64,8320]{1,0:T(8,128)(2,1)S(1)} %collective-permute-done.5.refs_1_, bf16[64,8320]{1,0:T(8,128)(2,1)S(1)} %collective-permute-done.8.refs_2_, ...), custom_call_target="tpu_custom_call" | custom-call | flops 4294967296 | bytes 16777216 | tf_op jit(solution)/shard_map/score_group/pallas_call | solution.py:193
  84.7 2.7 %collective-permute-start.22 = (bf16[128,1152]{1,0:T(8,128)(2,1)S(1)}, bf16[128,1152]{1,0:T(8,128)(2,1)S(1)}, u32[]{:S(2)}, u32[]{:S(2)}) collective-permute-start(bf16[128,1152]{1,0:T(8,128)(2,1)S(1)} %get-tuple-element.62), channel_id=1, source_target_pairs={{0,4},{1,5},{2,6},{3,7},{4,0},{5,1},{6,2},{7,3},{8,12},{9,13},{10,... | collective-permute-start | bytes 884744 | tf_op jit(solution)/shard_map/over_oq/ppermute | solution.py:295
  87.4 5.4 %score_and_deal.3 = (bf16[128,1152]{1,0:T(8,128)(2,1)S(1)}, bf16[128,1152]{1,0:T(8,128)(2,1)S(1)}, bf16[128,1152]{1,0:T(8,128)(2,1)S(1)}, bf16[128,1152]{1,0:T(8,128)(2,1)S(1)}) custom-call(s32[15]{0:T(128)S(1)} %stack.55.place.which, bf16[64,8320]{1,0:T(8,128)(2,1)S(1)} %collective-permute-done.3.b.refs_0_, ...), custom_call_target="tpu_custom_call" | custom-call | flops 4294967296 | bytes 16777216 | tf_op jit(solution)/shard_map/score_and_deal/pallas_call | solution.py:193
  94.1 2.1 %collective-permute-start.20 = (bf16[128,1152]{1,0:T(8,128)(2,1)S(1)}, bf16[128,1152]{1,0:T(8,128)(2,1)S(1)}, u32[]{:S(2)}, u32[]{:S(2)}) collective-permute-start(bf16[128,1152]{1,0:T(8,128)(2,1)S(1)} %get-tuple-element.73), channel_id=1, source_target_pairs={{0,6},{1,7},{2,0},{3,1},{4,2},{5,3},{6,4},{7,5},{8,14},{9,15},{10,... | collective-permute-start | bytes 884744 | tf_op jit(solution)/shard_map/down_st/ppermute | solution.py:295
  97.5 5.6 %collective-permute-start.24 = (bf16[128,1152]{1,0:T(8,128)(2,1)S(1)}, bf16[128,1152]{1,0:T(8,128)(2,1)S(1)}, u32[]{:S(2)}, u32[]{:S(2)}) collective-permute-start(bf16[128,1152]{1,0:T(8,128)(2,1)S(1)} %get-tuple-element.80), channel_id=1, source_target_pairs={{1,0},{2,3},{5,4},{6,7},{9,8},{10,11},{13,12},{14,15},{16,17},{19,... | collective-permute-start | bytes 884744 | tf_op jit(solution)/shard_map/oq/ppermute | solution.py:295
  103.2 5.3 %collective-permute-done.20.b = bf16[128,1152]{1,0:T(8,128)(2,1)S(1)} collective-permute-done((bf16[128,1152]{1,0:T(8,128)(2,1)S(1)}, bf16[128,1152]{1,0:T(8,128)(2,1)S(1)}, u32[]{:S(2)}, u32[]{:S(2)}) %collective-permute-start.20) | collective-permute-done | bytes 294944 | tf_op jit(solution)/shard_map/down_st/ppermute | solution.py:295
  108.4 1.8 %collective-permute-done.21.c = bf16[128,1152]{1,0:T(8,128)(2,1)S(1)} collective-permute-done((bf16[128,1152]{1,0:T(8,128)(2,1)S(1)}, bf16[128,1152]{1,0:T(8,128)(2,1)S(1)}, u32[]{:S(2)}, u32[]{:S(2)}) %collective-permute-start.21) | collective-permute-done | bytes 294944 | tf_op jit(solution)/shard_map/over_st/ppermute | solution.py:295
  111.9 10.3 %collective-permute-done.23.got_0 = bf16[128,1152]{1,0:T(8,128)(2,1)S(1)} collective-permute-done((bf16[128,1152]{1,0:T(8,128)(2,1)S(1)}, bf16[128,1152]{1,0:T(8,128)(2,1)S(1)}, u32[]{:S(2)}, u32[]{:S(2)}) %collective-permute-start.23) | collective-permute-done | bytes 294944 | tf_op jit(solution)/shard_map/st/ppermute | solution.py:295
  (42 shorter events, 11.0 us)
Async XLA Ops:
  9.8 25.3 %collective-permute-start = (bf16[64,8320]{1,0:T(8,128)(2,1)S(1)}, bf16[64,8320]{1,0:T(8,128)(2,1)S(1)}, u32[]{:S(2)}, u32[]{:S(2)}) collective-permute-start(bf16[64,8320]{1,0:T(8,128)(2,1)S(1)} %condition.1.refs_0_), channel_id=1, source_target_pairs={{0,16},{8,24},{16,0},{24,8},{32,48},{40,56},{48,32},{56,40},{64,80... | collective-permute-start | bytes 3194888 | tf_op jit(solution)/shard_map/s0/ppermute | solution.py:291
  10.2 25.7 %collective-permute-start.1 = (bf16[64,8320]{1,0:T(8,128)(2,1)S(1)}, bf16[64,8320]{1,0:T(8,128)(2,1)S(1)}, u32[]{:S(2)}, u32[]{:S(2)}) collective-permute-start(bf16[64,8320]{1,0:T(8,128)(2,1)S(1)} %condition.1.refs_0_), channel_id=1, source_target_pairs={{0,48},{8,56},{16,32},{24,40},{32,16},{40,24},{48,0},{56,8},{64,11... | collective-permute-start | bytes 3194888 | tf_op jit(solution)/shard_map/q0/ppermute | solution.py:291
  12.6 24.9 %collective-permute-start.2 = (bf16[64,8320]{1,0:T(8,128)(2,1)S(1)}, bf16[64,8320]{1,0:T(8,128)(2,1)S(1)}, u32[]{:S(2)}, u32[]{:S(2)}) collective-permute-start(bf16[64,8320]{1,0:T(8,128)(2,1)S(1)} %condition.1.refs_0_), channel_id=1, source_target_pairs={{0,64},{8,72},{16,80},{24,88},{32,96},{40,104},{48,112},{56,120},{... | collective-permute-start | bytes 3194888 | tf_op jit(solution)/shard_map/o1/ppermute | solution.py:291
  14.6 27.5 %collective-permute-start.6 = (bf16[64,8320]{1,0:T(8,128)(2,1)S(1)}, bf16[64,8320]{1,0:T(8,128)(2,1)S(1)}, u32[]{:S(2)}, u32[]{:S(2)}) collective-permute-start(bf16[64,8320]{1,0:T(8,128)(2,1)S(1)} %condition.1.refs_0_), channel_id=1, source_target_pairs={{0,8},{8,0},{16,24},{24,16},{32,40},{40,32},{48,56},{56,48},{64,72... | collective-permute-start | bytes 3194888 | tf_op jit(solution)/shard_map/own_sib/ppermute | solution.py:291
  37.5 4.6 %collective-permute-start.7 = (bf16[64,8320]{1,0:T(8,128)(2,1)S(1)}, bf16[64,8320]{1,0:T(8,128)(2,1)S(1)}, u32[]{:S(2)}, u32[]{:S(2)}) collective-permute-start(bf16[64,8320]{1,0:T(8,128)(2,1)S(1)} %collective-permute-done.2.refs_1_), channel_id=1, source_target_pairs={{0,8},{8,0},{16,24},{24,16},{32,40},{40,32},{48,56},{56,48},{64,72... | collective-permute-start | bytes 3194888 | tf_op jit(solution)/shard_map/o1_sib/ppermute | solution.py:291
  37.5 26.6 %collective-permute-start.4 = (bf16[64,8320]{1,0:T(8,128)(2,1)S(1)}, bf16[64,8320]{1,0:T(8,128)(2,1)S(1)}, u32[]{:S(2)}, u32[]{:S(2)}) collective-permute-start(bf16[64,8320]{1,0:T(8,128)(2,1)S(1)} %collective-permute-done.2.refs_1_), channel_id=1, source_target_pairs={{0,48},{8,56},{16,32},{24,40},{32,16},{40,24},{48,0},{56,8},{64,11... | collective-permute-start | bytes 3194888 | tf_op jit(solution)/shard_map/q1/ppermute | solution.py:291
  37.8 26.3 %collective-permute-start.3 = (bf16[64,8320]{1,0:T(8,128)(2,1)S(1)}, bf16[64,8320]{1,0:T(8,128)(2,1)S(1)}, u32[]{:S(2)}, u32[]{:S(2)}) collective-permute-start(bf16[64,8320]{1,0:T(8,128)(2,1)S(1)} %collective-permute-done.1.refs_0_), channel_id=1, source_target_pairs={{0,16},{8,24},{16,0},{24,8},{32,48},{40,56},{48,32},{56,40},{64,80... | collective-permute-start | bytes 3194888 | tf_op jit(solution)/shard_map/t0/ppermute | solution.py:291
  40.2 25.5 %collective-permute-start.5 = (bf16[64,8320]{1,0:T(8,128)(2,1)S(1)}, bf16[64,8320]{1,0:T(8,128)(2,1)S(1)}, u32[]{:S(2)}, u32[]{:S(2)}) collective-permute-start(bf16[64,8320]{1,0:T(8,128)(2,1)S(1)} %collective-permute-done.refs_0_), channel_id=1, source_target_pairs={{0,64},{8,72},{16,80},{24,88},{32,96},{40,104},{48,112},{56,120},{... | collective-permute-start | bytes 3194888 | tf_op jit(solution)/shard_map/s1/ppermute | solution.py:291
  42.1 23.6 %collective-permute-start.8 = (bf16[64,8320]{1,0:T(8,128)(2,1)S(1)}, bf16[64,8320]{1,0:T(8,128)(2,1)S(1)}, u32[]{:S(2)}, u32[]{:S(2)}) collective-permute-start(bf16[64,8320]{1,0:T(8,128)(2,1)S(1)} %collective-permute-done.refs_0_), channel_id=1, source_target_pairs={{0,8},{8,0},{16,24},{24,16},{32,40},{40,32},{48,56},{56,48},{64,72... | collective-permute-start | bytes 3194888 | tf_op jit(solution)/shard_map/s0_sib/ppermute | solution.py:291
  42.1 26.0 %collective-permute-start.11 = (bf16[64,8320]{1,0:T(8,128)(2,1)S(1)}, bf16[64,8320]{1,0:T(8,128)(2,1)S(1)}, u32[]{:S(2)}, u32[]{:S(2)}) collective-permute-start(bf16[64,8320]{1,0:T(8,128)(2,1)S(1)} %collective-permute-done.1.refs_0_), channel_id=1, source_target_pairs={{0,8},{8,0},{16,24},{24,16},{32,40},{40,32},{48,56},{56,48},{64,72... | collective-permute-start | bytes 3194888 | tf_op jit(solution)/shard_map/q0_sib/ppermute | solution.py:291
  65.7 8.3 %collective-permute-start.13 = (bf16[64,8320]{1,0:T(8,128)(2,1)S(1)}, bf16[64,8320]{1,0:T(8,128)(2,1)S(1)}, u32[]{:S(2)}, u32[]{:S(2)}) collective-permute-start(bf16[64,8320]{1,0:T(8,128)(2,1)S(1)} %collective-permute-done.5.refs_1_), channel_id=1, source_target_pairs={{0,8},{8,0},{16,24},{24,16},{32,40},{40,32},{48,56},{56,48},{64,72... | collective-permute-start | bytes 3194888 | tf_op jit(solution)/shard_map/s1_sib/ppermute | solution.py:291
  66.2 7.8 %collective-permute-start.14 = (bf16[64,8320]{1,0:T(8,128)(2,1)S(1)}, bf16[64,8320]{1,0:T(8,128)(2,1)S(1)}, u32[]{:S(2)}, u32[]{:S(2)}) collective-permute-start(bf16[64,8320]{1,0:T(8,128)(2,1)S(1)} %collective-permute-done.3.b.refs_0_), channel_id=1, source_target_pairs={{0,8},{8,0},{16,24},{24,16},{32,40},{40,32},{48,56},{56,48},{64,72... | collective-permute-start | bytes 3194888 | tf_op jit(solution)/shard_map/t0_sib/ppermute | solution.py:291
  66.3 16.3 %collective-permute-start.10 = (bf16[32,8320]{1,0:T(8,128)(2,1)S(1)}, bf16[32,8320]{1,0:T(8,128)(2,1)S(1)}, u32[]{:S(2)}, u32[]{:S(2)}) collective-permute-start(bf16[32,8320]{1,0:T(8,128)(2,1)S(1)} %get-tuple-element.53), channel_id=1, source_target_pairs={{0,64},{8,72},{16,80},{24,88},{32,96},{40,104},{48,112},{56,120},{... | collective-permute-start | bytes 1597448 | tf_op jit(solution)/shard_map/t1b/ppermute | solution.py:291
  68.1 14.5 %collective-permute-start.9 = (bf16[32,8320]{1,0:T(8,128)(2,1)S(1)}, bf16[32,8320]{1,0:T(8,128)(2,1)S(1)}, u32[]{:S(2)}, u32[]{:S(2)}) collective-permute-start(bf16[32,8320]{1,0:T(8,128)(2,1)S(1)} %get-tuple-element.52), channel_id=1, source_target_pairs={{0,16},{8,24},{16,0},{24,8},{32,48},{40,56},{48,32},{56,40},{64,80... | collective-permute-start | bytes 1597448 | tf_op jit(solution)/shard_map/t1a/ppermute | solution.py:291
  74.0 10.1 %collective-permute-start.15 = (bf16[128,1152]{1,0:T(8,128)(2,1)S(1)}, bf16[128,1152]{1,0:T(8,128)(2,1)S(1)}, u32[]{:S(2)}, u32[]{:S(2)}) collective-permute-start(bf16[128,1152]{1,0:T(8,128)(2,1)S(1)} %get-tuple-element.61), channel_id=1, source_target_pairs={{0,2},{1,3},{2,4},{3,5},{4,6},{5,7},{6,0},{7,1},{8,10},{9,11},{10,... | collective-permute-start | bytes 884744 | tf_op jit(solution)/shard_map/up_oq/ppermute | solution.py:295
  75.6 8.6 %collective-permute-start.16 = (bf16[128,1152]{1,0:T(8,128)(2,1)S(1)}, bf16[128,1152]{1,0:T(8,128)(2,1)S(1)}, u32[]{:S(2)}, u32[]{:S(2)}) collective-permute-start(bf16[128,1152]{1,0:T(8,128)(2,1)S(1)} %get-tuple-element.63), channel_id=1, source_target_pairs={{0,6},{1,7},{2,0},{3,1},{4,2},{5,3},{6,4},{7,5},{8,14},{9,15},{10,... | collective-permute-start | bytes 884744 | tf_op jit(solution)/shard_map/down_oq/ppermute | solution.py:295
  84.2 3.2 %collective-permute-start.17 = (bf16[32,8320]{1,0:T(8,128)(2,1)S(1)}, bf16[32,8320]{1,0:T(8,128)(2,1)S(1)}, u32[]{:S(2)}, u32[]{:S(2)}) collective-permute-start(bf16[32,8320]{1,0:T(8,128)(2,1)S(1)} %collective-permute-done.9.refs_1_), channel_id=1, source_target_pairs={{0,8},{8,0},{16,24},{24,16},{32,40},{40,32},{48,56},{56,48},{64,72... | collective-permute-start | bytes 1597448 | tf_op jit(solution)/shard_map/t1a_sib/ppermute | solution.py:291
  84.2 3.2 %collective-permute-start.18 = (bf16[32,8320]{1,0:T(8,128)(2,1)S(1)}, bf16[32,8320]{1,0:T(8,128)(2,1)S(1)}, u32[]{:S(2)}, u32[]{:S(2)}) collective-permute-start(bf16[32,8320]{1,0:T(8,128)(2,1)S(1)} %collective-permute-done.10.refs_2_), channel_id=1, source_target_pairs={{0,8},{8,0},{16,24},{24,16},{32,40},{40,32},{48,56},{56,48},{64,72... | collective-permute-start | bytes 1597448 | tf_op jit(solution)/shard_map/t1b_sib/ppermute | solution.py:291
  84.7 12.4 %collective-permute-start.22 = (bf16[128,1152]{1,0:T(8,128)(2,1)S(1)}, bf16[128,1152]{1,0:T(8,128)(2,1)S(1)}, u32[]{:S(2)}, u32[]{:S(2)}) collective-permute-start(bf16[128,1152]{1,0:T(8,128)(2,1)S(1)} %get-tuple-element.62), channel_id=1, source_target_pairs={{0,4},{1,5},{2,6},{3,7},{4,0},{5,1},{6,2},{7,3},{8,12},{9,13},{10,... | collective-permute-start | bytes 884744 | tf_op jit(solution)/shard_map/over_oq/ppermute | solution.py:295
  92.9 10.3 %collective-permute-start.19 = (bf16[128,1152]{1,0:T(8,128)(2,1)S(1)}, bf16[128,1152]{1,0:T(8,128)(2,1)S(1)}, u32[]{:S(2)}, u32[]{:S(2)}) collective-permute-start(bf16[128,1152]{1,0:T(8,128)(2,1)S(1)} %get-tuple-element.72), channel_id=1, source_target_pairs={{0,2},{1,3},{2,4},{3,5},{4,6},{5,7},{6,0},{7,1},{8,10},{9,11},{10,... | collective-permute-start | bytes 884744 | tf_op jit(solution)/shard_map/up_st/ppermute | solution.py:295
  94.1 14.3 %collective-permute-start.20 = (bf16[128,1152]{1,0:T(8,128)(2,1)S(1)}, bf16[128,1152]{1,0:T(8,128)(2,1)S(1)}, u32[]{:S(2)}, u32[]{:S(2)}) collective-permute-start(bf16[128,1152]{1,0:T(8,128)(2,1)S(1)} %get-tuple-element.73), channel_id=1, source_target_pairs={{0,6},{1,7},{2,0},{3,1},{4,2},{5,3},{6,4},{7,5},{8,14},{9,15},{10,... | collective-permute-start | bytes 884744 | tf_op jit(solution)/shard_map/down_st/ppermute | solution.py:295
  96.2 14.1 %collective-permute-start.21 = (bf16[128,1152]{1,0:T(8,128)(2,1)S(1)}, bf16[128,1152]{1,0:T(8,128)(2,1)S(1)}, u32[]{:S(2)}, u32[]{:S(2)}) collective-permute-start(bf16[128,1152]{1,0:T(8,128)(2,1)S(1)} %get-tuple-element.74), channel_id=1, source_target_pairs={{0,4},{1,5},{2,6},{3,7},{4,0},{5,1},{6,2},{7,3},{8,12},{9,13},{10,... | collective-permute-start | bytes 884744 | tf_op jit(solution)/shard_map/over_st/ppermute | solution.py:295
  97.5 14.4 %collective-permute-start.24 = (bf16[128,1152]{1,0:T(8,128)(2,1)S(1)}, bf16[128,1152]{1,0:T(8,128)(2,1)S(1)}, u32[]{:S(2)}, u32[]{:S(2)}) collective-permute-start(bf16[128,1152]{1,0:T(8,128)(2,1)S(1)} %get-tuple-element.80), channel_id=1, source_target_pairs={{1,0},{2,3},{5,4},{6,7},{9,8},{10,11},{13,12},{14,15},{16,17},{19,... | collective-permute-start | bytes 884744 | tf_op jit(solution)/shard_map/oq/ppermute | solution.py:295
  110.6 11.6 %collective-permute-start.23 = (bf16[128,1152]{1,0:T(8,128)(2,1)S(1)}, bf16[128,1152]{1,0:T(8,128)(2,1)S(1)}, u32[]{:S(2)}, u32[]{:S(2)}) collective-permute-start(bf16[128,1152]{1,0:T(8,128)(2,1)S(1)} %get-tuple-element.79), channel_id=1, source_target_pairs={{0,1},{3,2},{4,5},{7,6},{8,9},{11,10},{12,13},{15,14},{17,16},{18,... | collective-permute-start | bytes 884744 | tf_op jit(solution)/shard_map/st/ppermute | solution.py:295
  (3 other events, 6.7 us)

commit v2 on v1

--- a/solution.py
+++ b/solution.py
@@ -161,20 +161,29 @@
     scores[:, edge:] = group[:, stored.shape[1] :]
 
 
-def deal_kernel(at, deal, place, *refs):
-    *pieces, stored, before, o0, o1, o2, o3, group, blocks = refs
+def deal_kernel(at, deal, parts, count, place, *refs):
+    pieces, stored, before = refs[:count], refs[count], refs[count + 1]
+    outs, (group, blocks) = refs[count + 2 : -2], refs[-2:]
     edge = before.shape[1] - PAD
     rows = before.shape[0]
     fill(at, place, pieces, group)
     blocks[:rows] = before[...]
     blocks[rows:, :edge] = products(group, stored).astype(BF)
     blocks[rows:, edge:] = group[:, stored.shape[1] :]
-    for j, out in enumerate((o0, o1, o2, o3)):
-        start = pl.multiple_of(place[deal + j] * out.shape[0], 128)
-        out[...] = blocks[pl.ds(start, out.shape[0]), :]
-
-
-def score_group(place, at, pieces, stored, before=None, deal=None):
+    size = rows // 2
+    for j in range(4):
+        take = pl.ds(pl.multiple_of(place[deal + j] * size, 128), size)
+        if parts == 1:
+            outs[j][...] = blocks[take, :]
+        else:
+            first, second = outs[2 * j], outs[2 * j + 1]
+            cut = second.shape[1]
+            first[:, :cut] = blocks[take, :cut]
+            first[:, cut:] = blocks[take, edge:]
+            second[...] = blocks[take, cut:edge]
+
+
+def score_group(place, at, pieces, stored, before=None, deal=None, parts=1):
     count, width = stored.shape
     rows = sum(p.shape[0] for p in pieces)
     vmem = pl.BlockSpec(memory_space=pltpu.VMEM)
@@ -185,9 +194,10 @@
         kernel, name = functools.partial(score_kernel, at), "score_group"
         out, out_specs = shape, vmem
     else:
-        kernel, name = functools.partial(deal_kernel, at, deal), "score_and_deal"
-        out = [jax.ShapeDtypeStruct((rows // 2, count + PAD), BF)] * 4
-        out_specs = [vmem] * 4
+        kernel, name = functools.partial(deal_kernel, at, deal, parts, len(pieces)), "score_and_deal"
+        widths = [count + PAD] if parts == 1 else [count // 2 + PAD, count // 2]
+        out = [jax.ShapeDtypeStruct((rows // 2, w), BF) for w in widths] * 4
+        out_specs = [vmem] * len(out)
         scratch.append(pltpu.VMEM((2 * rows, count + PAD), BF))
         more = [before]
     return pl.pallas_call(
@@ -214,11 +224,17 @@
     onward[:, edge:] = norm_columns(norms)
 
 
-def sum_blocks(blocks):
+def plain_kernel(v, a, b, c, keep, onward):
+    total = v[...].astype(F32) + a[...].astype(F32) + b[...].astype(F32) + c[...].astype(F32)
+    keep[...] = total
+    onward[...] = total.astype(BF)
+
+
+def sum_blocks(blocks, with_norms=True):
     shape = blocks[0].shape
     vmem = pl.BlockSpec(memory_space=pltpu.VMEM)
     return pl.pallas_call(
-        sum_kernel,
+        sum_kernel if with_norms else plain_kernel,
         out_shape=(jax.ShapeDtypeStruct(shape, F32), jax.ShapeDtypeStruct(shape, BF)),
         in_specs=[vmem] * 4,
         out_specs=(vmem, vmem),
@@ -227,31 +243,38 @@
     )(*blocks)
 
 
-def finish_kernel(at, which, keep_0, keep_1, got_0, got_1, out):
-    edge = out.shape[1]
-
-    def write(keep, got):
-        more = got[...].astype(F32)
-        norms = keep[:, edge : edge + 1] + (
-            more[:, edge : edge + 1] + more[:, edge + PAD // 2 : edge + PAD // 2 + 1]
-        )
-        out[...] = (keep[:, :edge] + more[:, :edge]) * lax.rsqrt(norms + EPS)
-
-    pl.when(which[at] == 0)(lambda: write(keep_0, got_0))
-    pl.when(which[at] != 0)(lambda: write(keep_1, got_1))
-
-
-def finish(which, at, keeps, gots):
-    rows, width = keeps[0].shape
+def finish_kernel(at, which, *refs):
+    *parts, out = refs
+
+    def scale(keep, got):
+        edge = keep.shape[1] - PAD
+        more = got[:, edge:].astype(F32)
+        norms = keep[:, edge : edge + 1] + (more[:, :1] + more[:, PAD // 2 : PAD // 2 + 1])
+        return lax.rsqrt(norms + EPS)
+
+    def write(pairs):
+        by = scale(*pairs[0])
+        start = 0
+        for i, (keep, got) in enumerate(pairs):
+            stop = start + keep.shape[1] - (PAD if i == 0 else 0)
+            out[:, start:stop] = (keep[:, : stop - start] + got[:, : stop - start].astype(F32)) * by
+            start = stop
+
+    pl.when(which[at] == 0)(lambda: write([parts[0:2], parts[2:4]]))
+    pl.when(which[at] != 0)(lambda: write([parts[4:6]]))
+
+
+def finish(which, at, late, early, columns):
     vmem = pl.BlockSpec(memory_space=pltpu.VMEM)
+    arrays = [array for pair in (*late, *early) for array in pair]
     return pl.pallas_call(
         functools.partial(finish_kernel, at),
-        out_shape=jax.ShapeDtypeStruct((rows, width - PAD), F32),
-        in_specs=[pl.BlockSpec(memory_space=pltpu.SMEM)] + [vmem] * 4,
+        out_shape=jax.ShapeDtypeStruct((arrays[0].shape[0], columns), F32),
+        in_specs=[pl.BlockSpec(memory_space=pltpu.SMEM)] + [vmem] * len(arrays),
         out_specs=vmem,
         compiler_params=pltpu.CompilerParams(vmem_limit_bytes=4 * MIB),
         name="finish",
-    )(which, *keeps, *gots)
+    )(which, *arrays)
 
 
 def split_kernel(a, b, first, second):
@@ -349,19 +372,25 @@
     t1a_sib, t1b_sib = send(t1a, SIBLING, "t1a_sib"), send(t1b, SIBLING, "t1b_sib")
     keep_1, onward_1 = sum_blocks([mine, up, down, over])
     last = [t0, t1a, t1b, t0_sib, t1a_sib, t1b_sib]
-    dealt_2 = score_group(table, starts[2], last, stored, scores_s, starts[1])
-    keep_2, onward_2 = sum_blocks(reduce_batch(dealt_2, "_st"))
+    dealt_2 = score_group(
+        table, starts[2], last, stored, scores_s, starts[1], parts=2
+    )
+    keep_2, onward_2 = sum_blocks(reduce_batch(dealt_2[0::2], "_st"))
+    keep_3, onward_3 = sum_blocks(reduce_batch(dealt_2[1::2], "_st_right"), with_norms=False)
 
     def final_first(yy, xx, hh):
         return (xx % 2 == yy // 2) == (hh == yy % 2)
+
+    def other(zz, yy, xx, hh):
+        return (xx, 1 - hh) if final_first(yy, xx, hh) else None
 
     got_1 = whole(
         onward_1, lambda zz, yy, xx, hh: None if final_first(yy, xx, hh) else (xx, 1 - hh), "oq"
     )
-    got_2 = whole(
-        onward_2, lambda zz, yy, xx, hh: (xx, 1 - hh) if final_first(yy, xx, hh) else None, "st"
-    )
-    return finish(table, starts[3], [keep_2, keep_1], [got_2, got_1])
+    got_2 = whole(onward_2, other, "st")
+    got_3 = whole(onward_3, other, "st_right")
+    late = [(keep_2, got_2), (keep_3, got_3)]
+    return finish(table, starts[3], late, [(keep_1, got_1)], row_count)
 
 
 def solution(mesh):

time: 125 us -> 123 us (0.984)
  waiting for transfers between devices: 45 us -> 38.2 us
  starting transfers between devices: 30.4 us -> 36.4 us
    ppermute x8 -> x12, waiting for transfers between devices: 18.9 us -> 12.1 us  [whole(): return lax.ppermute(value, BOTH, whole_perm(move))]
    ppermute x8 -> x12, starting transfers between devices: 17.2 us -> 23.2 us  [whole(): return lax.ppermute(value, BOTH, whole_perm(move))]
  transfers between devices with their start and end apart: 25 -> 29, of which waited for: 9 -> 10; matrix products, arithmetic and copies ran while one was open for 12% -> 12% of each run, Pallas kernels for 18% -> 18%
where the time goes in v2:
time: 123 us
  waiting for transfers between devices  38.2 us (31%)
  starting transfers between devices  36.4 us (30%)
  Pallas kernels  31.6 us (26%)
  local copies, waits for them, and re-layouts  16.6 us (13%)
    ppermute x17, waiting for transfers between devices, send(): return lax.ppermute(value, 'rows', pairs)  26.1 us
    ppermute x12, starting transfers between devices, whole(): return lax.ppermute(value, BOTH, whole_perm(move))  23.2 us
    pallas_call x4, Pallas kernels, score_group(): pl.pallas_call(kernel, out_shape=out, in_specs=[pl.BlockSpec(memory_space...  21.4 us
    unnamed x5, local copies, waits for them, and re-layouts  14.7 us
    ppermute x17, starting transfers between devices, send(): return lax.ppermute(value, 'rows', pairs)  13.2 us
    ppermute x12, waiting for transfers between devices, whole(): return lax.ppermute(value, BOTH, whole_perm(move))  12.1 us
    pallas_call x1, Pallas kernels, condition(): pl.pallas_call(condition_kernel, out_shape=jax.ShapeDtypeStruct((count, l...  7.84 us
  transfers between devices with their start and end apart: 29, of which 10 were waited for; matrix products, arithmetic and copies ran while one was open for 12% of the time, Pallas kernels for 18%

profile of v2, /device:TPU:8, one launch (start us, length us, event | category | flops | bytes accessed | tf_op | source)
XLA Modules:
  0.0 122.9 jit_solution(2547475686323512291)
XLA Ops:
  0.1 1.8 %copy.8 = bf16[64,2,4096]{2,0,1:T(8,128)(2,1)S(1)} copy(bf16[64,2,4096]{2,1,0:T(2,128)(2,1)} %param.4) | data formatting | bytes 2097152 | tf_op jit(solution)/shard_map/optimization_barrier | solution.py:348
  1.9 7.8 %condition.1.refs_0_ = bf16[64,8320]{1,0:T(8,128)(2,1)S(1)} custom-call(bf16[2,64,4096]{2,1,0:T(8,128)(2,1)S(1)} %bitcast.20, f32[2,64,64]{2,1,0:T(8,128)S(1)} %copy-done, f32[2,64,64]{2,1,0:T(8,128)S(1)} %copy-done.1), custom_call_target="tpu_custom_call" | custom-call | tf_op jit(solution)/shard_map/condition/pallas_call | solution.py:128
  10.2 2.5 %collective-permute-start.1 = (bf16[64,8320]{1,0:T(8,128)(2,1)S(1)}, bf16[64,8320]{1,0:T(8,128)(2,1)S(1)}, u32[]{:S(2)}, u32[]{:S(2)}) collective-permute-start(bf16[64,8320]{1,0:T(8,128)(2,1)S(1)} %condition.1.refs_0_), channel_id=1, source_target_pairs={{0,48},{8,56},{16,32},{24,40},{32,16},{40,24},{48,0},{56,8},{64,11... | collective-permute-start | bytes 3194888 | tf_op jit(solution)/shard_map/q0/ppermute | solution.py:314
  12.6 1.9 %collective-permute-start.2 = (bf16[64,8320]{1,0:T(8,128)(2,1)S(1)}, bf16[64,8320]{1,0:T(8,128)(2,1)S(1)}, u32[]{:S(2)}, u32[]{:S(2)}) collective-permute-start(bf16[64,8320]{1,0:T(8,128)(2,1)S(1)} %condition.1.refs_0_), channel_id=1, source_target_pairs={{0,64},{8,72},{16,80},{24,88},{32,96},{40,104},{48,112},{56,120},{... | collective-permute-start | bytes 3194888 | tf_op jit(solution)/shard_map/o1/ppermute | solution.py:314
  14.6 14.7 %copy.6 = bf16[128,8,2,4096]{3,1,2,0:T(8,128)(2,1)S(1)} copy(bf16[128,8,2,4096]{3,2,1,0:T(2,128)(2,1)} %bitcast.21) | data formatting | bytes 33554432
  29.3 5.8 %collective-permute-done.refs_0_ = bf16[64,8320]{1,0:T(8,128)(2,1)S(1)} collective-permute-done((bf16[64,8320]{1,0:T(8,128)(2,1)S(1)}, bf16[64,8320]{1,0:T(8,128)(2,1)S(1)}, u32[]{:S(2)}, u32[]{:S(2)}) %collective-permute-start) | collective-permute-done | bytes 1064992 | tf_op jit(solution)/shard_map/s0/ppermute | solution.py:314
  35.9 1.6 %collective-permute-done.2.refs_1_ = bf16[64,8320]{1,0:T(8,128)(2,1)S(1)} collective-permute-done((bf16[64,8320]{1,0:T(8,128)(2,1)S(1)}, bf16[64,8320]{1,0:T(8,128)(2,1)S(1)}, u32[]{:S(2)}, u32[]{:S(2)}) %collective-permute-start.2) | collective-permute-done | bytes 1064992 | tf_op jit(solution)/shard_map/o1/ppermute | solution.py:314
  37.8 2.4 %collective-permute-start.3 = (bf16[64,8320]{1,0:T(8,128)(2,1)S(1)}, bf16[64,8320]{1,0:T(8,128)(2,1)S(1)}, u32[]{:S(2)}, u32[]{:S(2)}) collective-permute-start(bf16[64,8320]{1,0:T(8,128)(2,1)S(1)} %collective-permute-done.1.refs_0_), channel_id=1, source_target_pairs={{0,16},{8,24},{16,0},{24,8},{32,48},{40,56},{48,32},{56,40},{64,80... | collective-permute-start | bytes 3194888 | tf_op jit(solution)/shard_map/t0/ppermute | solution.py:314
  40.2 1.9 %collective-permute-start.5 = (bf16[64,8320]{1,0:T(8,128)(2,1)S(1)}, bf16[64,8320]{1,0:T(8,128)(2,1)S(1)}, u32[]{:S(2)}, u32[]{:S(2)}) collective-permute-start(bf16[64,8320]{1,0:T(8,128)(2,1)S(1)} %collective-permute-done.refs_0_), channel_id=1, source_target_pairs={{0,64},{8,72},{16,80},{24,88},{32,96},{40,104},{48,112},{56,120},{... | collective-permute-start | bytes 3194888 | tf_op jit(solution)/shard_map/s1/ppermute | solution.py:314
  42.6 5.3 %score_group.2.refs_5_ = bf16[256,1152]{1,0:T(8,128)(2,1)S(1)} custom-call(s32[15]{0:T(128)S(1)} %stack.55.place.which, bf16[64,8320]{1,0:T(8,128)(2,1)S(1)} %condition.1.refs_0_, bf16[64,8320]{1,0:T(8,128)(2,1)S(1)} %collective-permute-done.2.refs_1_, bf16[64,8320]{1,0:T(8,128)(2,1)S(1)} %collective-permute-done.6.refs_2_, ...), custom_call_target="tpu_custom_call" | custom-call | flops 4294967296 | bytes 16777216 | tf_op jit(solution)/shard_map/score_group/pallas_call | solution.py:203
  47.9 16.2 %collective-permute-done.3.b.refs_0_ = bf16[64,8320]{1,0:T(8,128)(2,1)S(1)} collective-permute-done((bf16[64,8320]{1,0:T(8,128)(2,1)S(1)}, bf16[64,8320]{1,0:T(8,128)(2,1)S(1)}, u32[]{:S(2)}, u32[]{:S(2)}) %collective-permute-start.3) | collective-permute-done | bytes 1064992 | tf_op jit(solution)/shard_map/t0/ppermute | solution.py:314
  64.1 1.6 %collective-permute-done.5.refs_1_ = bf16[64,8320]{1,0:T(8,128)(2,1)S(1)} collective-permute-done((bf16[64,8320]{1,0:T(8,128)(2,1)S(1)}, bf16[64,8320]{1,0:T(8,128)(2,1)S(1)}, u32[]{:S(2)}, u32[]{:S(2)}) %collective-permute-start.5) | collective-permute-done | bytes 1064992 | tf_op jit(solution)/shard_map/s1/ppermute | solution.py:314
  66.3 1.8 %collective-permute-start.10 = (bf16[32,8320]{1,0:T(8,128)(2,1)S(1)}, bf16[32,8320]{1,0:T(8,128)(2,1)S(1)}, u32[]{:S(2)}, u32[]{:S(2)}) collective-permute-start(bf16[32,8320]{1,0:T(8,128)(2,1)S(1)} %get-tuple-element.59), channel_id=1, source_target_pairs={{0,64},{8,72},{16,80},{24,88},{32,96},{40,104},{48,112},{56,120},{... | collective-permute-start | bytes 1597448 | tf_op jit(solution)/shard_map/t1b/ppermute | solution.py:314
  68.6 5.4 %score_and_deal.2 = (bf16[128,1152]{1,0:T(8,128)(2,1)S(1)}, bf16[128,1152]{1,0:T(8,128)(2,1)S(1)}, bf16[128,1152]{1,0:T(8,128)(2,1)S(1)}, bf16[128,1152]{1,0:T(8,128)(2,1)S(1)}) custom-call(s32[15]{0:T(128)S(1)} %stack.55.place.which, bf16[64,8320]{1,0:T(8,128)(2,1)S(1)} %collective-permute-done.1.refs_0_, ...), custom_call_target="tpu_custom_call" | custom-call | flops 4294967296 | bytes 16777216 | tf_op jit(solution)/shard_map/score_and_deal/pallas_call | solution.py:203
  74.0 1.6 %collective-permute-start.15 = (bf16[128,1152]{1,0:T(8,128)(2,1)S(1)}, bf16[128,1152]{1,0:T(8,128)(2,1)S(1)}, u32[]{:S(2)}, u32[]{:S(2)}) collective-permute-start(bf16[128,1152]{1,0:T(8,128)(2,1)S(1)} %get-tuple-element.67), channel_id=1, source_target_pairs={{0,2},{1,3},{2,4},{3,5},{4,6},{5,7},{6,0},{7,1},{8,10},{9,11},{10,... | collective-permute-start | bytes 884744 | tf_op jit(solution)/shard_map/up_oq/ppermute | solution.py:318
  75.6 1.7 %collective-permute-start.16 = (bf16[128,1152]{1,0:T(8,128)(2,1)S(1)}, bf16[128,1152]{1,0:T(8,128)(2,1)S(1)}, u32[]{:S(2)}, u32[]{:S(2)}) collective-permute-start(bf16[128,1152]{1,0:T(8,128)(2,1)S(1)} %get-tuple-element.69), channel_id=1, source_target_pairs={{0,6},{1,7},{2,0},{3,1},{4,2},{5,3},{6,4},{7,5},{8,14},{9,15},{10,... | collective-permute-start | bytes 884744 | tf_op jit(solution)/shard_map/down_oq/ppermute | solution.py:318
  77.3 5.3 %score_group.3.refs_7_ = bf16[256,1152]{1,0:T(8,128)(2,1)S(1)} custom-call(s32[15]{0:T(128)S(1)} %stack.55.place.which, bf16[64,8320]{1,0:T(8,128)(2,1)S(1)} %collective-permute-done.refs_0_, bf16[64,8320]{1,0:T(8,128)(2,1)S(1)} %collective-permute-done.5.refs_1_, bf16[64,8320]{1,0:T(8,128)(2,1)S(1)} %collective-permute-done.8.refs_2_, ...), custom_call_target="tpu_custom_call" | custom-call | flops 4294967296 | bytes 16777216 | tf_op jit(solution)/shard_map/score_group/pallas_call | solution.py:203
  84.7 2.7 %collective-permute-start.27 = (bf16[128,1152]{1,0:T(8,128)(2,1)S(1)}, bf16[128,1152]{1,0:T(8,128)(2,1)S(1)}, u32[]{:S(2)}, u32[]{:S(2)}) collective-permute-start(bf16[128,1152]{1,0:T(8,128)(2,1)S(1)} %get-tuple-element.68), channel_id=1, source_target_pairs={{0,4},{1,5},{2,6},{3,7},{4,0},{5,1},{6,2},{7,3},{8,12},{9,13},{10,... | collective-permute-start | bytes 884744 | tf_op jit(solution)/shard_map/over_oq/ppermute | solution.py:318
  87.4 5.4 %score_and_deal.3 = (bf16[128,640]{1,0:T(8,128)(2,1)S(1)}, bf16[128,512]{1,0:T(8,128)(2,1)S(1)}, bf16[128,640]{1,0:T(8,128)(2,1)S(1)}, bf16[128,512]{1,0:T(8,128...) custom-call(s32[15]{0:T(128)S(1)} %stack.55.place.which, ...), custom_call_target="tpu_custom_call" | custom-call | flops 4294967296 | bytes 16777216 | tf_op jit(solution)/shard_map/score_and_deal/pallas_call | solution.py:203
  94.1 2.1 %collective-permute-start.20 = (bf16[128,640]{1,0:T(8,128)(2,1)S(1)}, bf16[128,640]{1,0:T(8,128)(2,1)S(1)}, u32[]{:S(2)}, u32[]{:S(2)}) collective-permute-start(bf16[128,640]{1,0:T(8,128)(2,1)S(1)} %get-tuple-element.79), channel_id=1, source_target_pairs={{0,6},{1,7},{2,0},{3,1},{4,2},{5,3},{6,4},{7,5},{8,14},{9,15},{10,... | collective-permute-start | bytes 491528 | tf_op jit(solution)/shard_map/down_st/ppermute | solution.py:318
  97.5 5.6 %collective-permute-start.28 = (bf16[128,1152]{1,0:T(8,128)(2,1)S(1)}, bf16[128,1152]{1,0:T(8,128)(2,1)S(1)}, u32[]{:S(2)}, u32[]{:S(2)}) collective-permute-start(bf16[128,1152]{1,0:T(8,128)(2,1)S(1)} %get-tuple-element.92), channel_id=1, source_target_pairs={{1,0},{2,3},{5,4},{6,7},{9,8},{10,11},{13,12},{14,15},{16,17},{19,... | collective-permute-start | bytes 884744 | tf_op jit(solution)/shard_map/oq/ppermute | solution.py:318
  103.3 3.2 %collective-permute-start.24 = (bf16[128,512]{1,0:T(8,128)(2,1)S(1)}, bf16[128,512]{1,0:T(8,128)(2,1)S(1)}, u32[]{:S(2)}, u32[]{:S(2)}) collective-permute-start(bf16[128,512]{1,0:T(8,128)(2,1)S(1)} %get-tuple-element.85), channel_id=1, source_target_pairs={{0,6},{1,7},{2,0},{3,1},{4,2},{5,3},{6,4},{7,5},{8,14},{9,15},{10,... | collective-permute-start | bytes 393224 | tf_op jit(solution)/shard_map/down_st_right/ppermute | solution.py:318
  111.0 1.9 %collective-permute-done.25.c = bf16[128,512]{1,0:T(8,128)(2,1)S(1)} collective-permute-done((bf16[128,512]{1,0:T(8,128)(2,1)S(1)}, bf16[128,512]{1,0:T(8,128)(2,1)S(1)}, u32[]{:S(2)}, u32[]{:S(2)}) %collective-permute-start.25) | collective-permute-done | bytes 131104 | tf_op jit(solution)/shard_map/over_st_right/ppermute | solution.py:318
  114.3 7.1 %collective-permute-done.26.refs_3_ = bf16[128,512]{1,0:T(8,128)(2,1)S(1)} collective-permute-done((bf16[128,512]{1,0:T(8,128)(2,1)S(1)}, bf16[128,512]{1,0:T(8,128)(2,1)S(1)}, u32[]{:S(2)}, u32[]{:S(2)}) %collective-permute-start.26) | collective-permute-done | bytes 131104 | tf_op jit(solution)/shard_map/st_right/ppermute | solution.py:318
  (51 shorter events, 15.3 us)
Async XLA Ops:
  9.8 25.3 %collective-permute-start = (bf16[64,8320]{1,0:T(8,128)(2,1)S(1)}, bf16[64,8320]{1,0:T(8,128)(2,1)S(1)}, u32[]{:S(2)}, u32[]{:S(2)}) collective-permute-start(bf16[64,8320]{1,0:T(8,128)(2,1)S(1)} %condition.1.refs_0_), channel_id=1, source_target_pairs={{0,16},{8,24},{16,0},{24,8},{32,48},{40,56},{48,32},{56,40},{64,80... | collective-permute-start | bytes 3194888 | tf_op jit(solution)/shard_map/s0/ppermute | solution.py:314
  10.2 25.7 %collective-permute-start.1 = (bf16[64,8320]{1,0:T(8,128)(2,1)S(1)}, bf16[64,8320]{1,0:T(8,128)(2,1)S(1)}, u32[]{:S(2)}, u32[]{:S(2)}) collective-permute-start(bf16[64,8320]{1,0:T(8,128)(2,1)S(1)} %condition.1.refs_0_), channel_id=1, source_target_pairs={{0,48},{8,56},{16,32},{24,40},{32,16},{40,24},{48,0},{56,8},{64,11... | collective-permute-start | bytes 3194888 | tf_op jit(solution)/shard_map/q0/ppermute | solution.py:314
  12.6 24.9 %collective-permute-start.2 = (bf16[64,8320]{1,0:T(8,128)(2,1)S(1)}, bf16[64,8320]{1,0:T(8,128)(2,1)S(1)}, u32[]{:S(2)}, u32[]{:S(2)}) collective-permute-start(bf16[64,8320]{1,0:T(8,128)(2,1)S(1)} %condition.1.refs_0_), channel_id=1, source_target_pairs={{0,64},{8,72},{16,80},{24,88},{32,96},{40,104},{48,112},{56,120},{... | collective-permute-start | bytes 3194888 | tf_op jit(solution)/shard_map/o1/ppermute | solution.py:314
  14.6 27.5 %collective-permute-start.6 = (bf16[64,8320]{1,0:T(8,128)(2,1)S(1)}, bf16[64,8320]{1,0:T(8,128)(2,1)S(1)}, u32[]{:S(2)}, u32[]{:S(2)}) collective-permute-start(bf16[64,8320]{1,0:T(8,128)(2,1)S(1)} %condition.1.refs_0_), channel_id=1, source_target_pairs={{0,8},{8,0},{16,24},{24,16},{32,40},{40,32},{48,56},{56,48},{64,72... | collective-permute-start | bytes 3194888 | tf_op jit(solution)/shard_map/own_sib/ppermute | solution.py:314
  37.5 26.6 %collective-permute-start.4 = (bf16[64,8320]{1,0:T(8,128)(2,1)S(1)}, bf16[64,8320]{1,0:T(8,128)(2,1)S(1)}, u32[]{:S(2)}, u32[]{:S(2)}) collective-permute-start(bf16[64,8320]{1,0:T(8,128)(2,1)S(1)} %collective-permute-done.2.refs_1_), channel_id=1, source_target_pairs={{0,48},{8,56},{16,32},{24,40},{32,16},{40,24},{48,0},{56,8},{64,11... | collective-permute-start | bytes 3194888 | tf_op jit(solution)/shard_map/q1/ppermute | solution.py:314
  37.8 26.3 %collective-permute-start.3 = (bf16[64,8320]{1,0:T(8,128)(2,1)S(1)}, bf16[64,8320]{1,0:T(8,128)(2,1)S(1)}, u32[]{:S(2)}, u32[]{:S(2)}) collective-permute-start(bf16[64,8320]{1,0:T(8,128)(2,1)S(1)} %collective-permute-done.1.refs_0_), channel_id=1, source_target_pairs={{0,16},{8,24},{16,0},{24,8},{32,48},{40,56},{48,32},{56,40},{64,80... | collective-permute-start | bytes 3194888 | tf_op jit(solution)/shard_map/t0/ppermute | solution.py:314
  40.2 25.5 %collective-permute-start.5 = (bf16[64,8320]{1,0:T(8,128)(2,1)S(1)}, bf16[64,8320]{1,0:T(8,128)(2,1)S(1)}, u32[]{:S(2)}, u32[]{:S(2)}) collective-permute-start(bf16[64,8320]{1,0:T(8,128)(2,1)S(1)} %collective-permute-done.refs_0_), channel_id=1, source_target_pairs={{0,64},{8,72},{16,80},{24,88},{32,96},{40,104},{48,112},{56,120},{... | collective-permute-start | bytes 3194888 | tf_op jit(solution)/shard_map/s1/ppermute | solution.py:314
  42.1 23.6 %collective-permute-start.8 = (bf16[64,8320]{1,0:T(8,128)(2,1)S(1)}, bf16[64,8320]{1,0:T(8,128)(2,1)S(1)}, u32[]{:S(2)}, u32[]{:S(2)}) collective-permute-start(bf16[64,8320]{1,0:T(8,128)(2,1)S(1)} %collective-permute-done.refs_0_), channel_id=1, source_target_pairs={{0,8},{8,0},{16,24},{24,16},{32,40},{40,32},{48,56},{56,48},{64,72... | collective-permute-start | bytes 3194888 | tf_op jit(solution)/shard_map/s0_sib/ppermute | solution.py:314
  42.1 26.0 %collective-permute-start.11 = (bf16[64,8320]{1,0:T(8,128)(2,1)S(1)}, bf16[64,8320]{1,0:T(8,128)(2,1)S(1)}, u32[]{:S(2)}, u32[]{:S(2)}) collective-permute-start(bf16[64,8320]{1,0:T(8,128)(2,1)S(1)} %collective-permute-done.1.refs_0_), channel_id=1, source_target_pairs={{0,8},{8,0},{16,24},{24,16},{32,40},{40,32},{48,56},{56,48},{64,72... | collective-permute-start | bytes 3194888 | tf_op jit(solution)/shard_map/q0_sib/ppermute | solution.py:314
  65.7 8.3 %collective-permute-start.13 = (bf16[64,8320]{1,0:T(8,128)(2,1)S(1)}, bf16[64,8320]{1,0:T(8,128)(2,1)S(1)}, u32[]{:S(2)}, u32[]{:S(2)}) collective-permute-start(bf16[64,8320]{1,0:T(8,128)(2,1)S(1)} %collective-permute-done.5.refs_1_), channel_id=1, source_target_pairs={{0,8},{8,0},{16,24},{24,16},{32,40},{40,32},{48,56},{56,48},{64,72... | collective-permute-start | bytes 3194888 | tf_op jit(solution)/shard_map/s1_sib/ppermute | solution.py:314
  66.2 7.8 %collective-permute-start.14 = (bf16[64,8320]{1,0:T(8,128)(2,1)S(1)}, bf16[64,8320]{1,0:T(8,128)(2,1)S(1)}, u32[]{:S(2)}, u32[]{:S(2)}) collective-permute-start(bf16[64,8320]{1,0:T(8,128)(2,1)S(1)} %collective-permute-done.3.b.refs_0_), channel_id=1, source_target_pairs={{0,8},{8,0},{16,24},{24,16},{32,40},{40,32},{48,56},{56,48},{64,72... | collective-permute-start | bytes 3194888 | tf_op jit(solution)/shard_map/t0_sib/ppermute | solution.py:314
  66.3 16.3 %collective-permute-start.10 = (bf16[32,8320]{1,0:T(8,128)(2,1)S(1)}, bf16[32,8320]{1,0:T(8,128)(2,1)S(1)}, u32[]{:S(2)}, u32[]{:S(2)}) collective-permute-start(bf16[32,8320]{1,0:T(8,128)(2,1)S(1)} %get-tuple-element.59), channel_id=1, source_target_pairs={{0,64},{8,72},{16,80},{24,88},{32,96},{40,104},{48,112},{56,120},{... | collective-permute-start | bytes 1597448 | tf_op jit(solution)/shard_map/t1b/ppermute | solution.py:314
  68.1 14.5 %collective-permute-start.9 = (bf16[32,8320]{1,0:T(8,128)(2,1)S(1)}, bf16[32,8320]{1,0:T(8,128)(2,1)S(1)}, u32[]{:S(2)}, u32[]{:S(2)}) collective-permute-start(bf16[32,8320]{1,0:T(8,128)(2,1)S(1)} %get-tuple-element.58), channel_id=1, source_target_pairs={{0,16},{8,24},{16,0},{24,8},{32,48},{40,56},{48,32},{56,40},{64,80... | collective-permute-start | bytes 1597448 | tf_op jit(solution)/shard_map/t1a/ppermute | solution.py:314
  74.0 10.1 %collective-permute-start.15 = (bf16[128,1152]{1,0:T(8,128)(2,1)S(1)}, bf16[128,1152]{1,0:T(8,128)(2,1)S(1)}, u32[]{:S(2)}, u32[]{:S(2)}) collective-permute-start(bf16[128,1152]{1,0:T(8,128)(2,1)S(1)} %get-tuple-element.67), channel_id=1, source_target_pairs={{0,2},{1,3},{2,4},{3,5},{4,6},{5,7},{6,0},{7,1},{8,10},{9,11},{10,... | collective-permute-start | bytes 884744 | tf_op jit(solution)/shard_map/up_oq/ppermute | solution.py:318
  75.6 8.6 %collective-permute-start.16 = (bf16[128,1152]{1,0:T(8,128)(2,1)S(1)}, bf16[128,1152]{1,0:T(8,128)(2,1)S(1)}, u32[]{:S(2)}, u32[]{:S(2)}) collective-permute-start(bf16[128,1152]{1,0:T(8,128)(2,1)S(1)} %get-tuple-element.69), channel_id=1, source_target_pairs={{0,6},{1,7},{2,0},{3,1},{4,2},{5,3},{6,4},{7,5},{8,14},{9,15},{10,... | collective-permute-start | bytes 884744 | tf_op jit(solution)/shard_map/down_oq/ppermute | solution.py:318
  84.7 12.4 %collective-permute-start.27 = (bf16[128,1152]{1,0:T(8,128)(2,1)S(1)}, bf16[128,1152]{1,0:T(8,128)(2,1)S(1)}, u32[]{:S(2)}, u32[]{:S(2)}) collective-permute-start(bf16[128,1152]{1,0:T(8,128)(2,1)S(1)} %get-tuple-element.68), channel_id=1, source_target_pairs={{0,4},{1,5},{2,6},{3,7},{4,0},{5,1},{6,2},{7,3},{8,12},{9,13},{10,... | collective-permute-start | bytes 884744 | tf_op jit(solution)/shard_map/over_oq/ppermute | solution.py:318
  92.9 10.4 %collective-permute-start.19 = (bf16[128,640]{1,0:T(8,128)(2,1)S(1)}, bf16[128,640]{1,0:T(8,128)(2,1)S(1)}, u32[]{:S(2)}, u32[]{:S(2)}) collective-permute-start(bf16[128,640]{1,0:T(8,128)(2,1)S(1)} %get-tuple-element.78), channel_id=1, source_target_pairs={{0,2},{1,3},{2,4},{3,5},{4,6},{5,7},{6,0},{7,1},{8,10},{9,11},{10,... | collective-permute-start | bytes 491528 | tf_op jit(solution)/shard_map/up_st/ppermute | solution.py:318
  94.1 12.4 %collective-permute-start.20 = (bf16[128,640]{1,0:T(8,128)(2,1)S(1)}, bf16[128,640]{1,0:T(8,128)(2,1)S(1)}, u32[]{:S(2)}, u32[]{:S(2)}) collective-permute-start(bf16[128,640]{1,0:T(8,128)(2,1)S(1)} %get-tuple-element.79), channel_id=1, source_target_pairs={{0,6},{1,7},{2,0},{3,1},{4,2},{5,3},{6,4},{7,5},{8,14},{9,15},{10,... | collective-permute-start | bytes 491528 | tf_op jit(solution)/shard_map/down_st/ppermute | solution.py:318
  96.2 11.7 %collective-permute-start.21 = (bf16[128,640]{1,0:T(8,128)(2,1)S(1)}, bf16[128,640]{1,0:T(8,128)(2,1)S(1)}, u32[]{:S(2)}, u32[]{:S(2)}) collective-permute-start(bf16[128,640]{1,0:T(8,128)(2,1)S(1)} %get-tuple-element.80), channel_id=1, source_target_pairs={{0,4},{1,5},{2,6},{3,7},{4,0},{5,1},{6,2},{7,3},{8,12},{9,13},{10,... | collective-permute-start | bytes 491528 | tf_op jit(solution)/shard_map/over_st/ppermute | solution.py:318
  97.5 16.8 %collective-permute-start.28 = (bf16[128,1152]{1,0:T(8,128)(2,1)S(1)}, bf16[128,1152]{1,0:T(8,128)(2,1)S(1)}, u32[]{:S(2)}, u32[]{:S(2)}) collective-permute-start(bf16[128,1152]{1,0:T(8,128)(2,1)S(1)} %get-tuple-element.92), channel_id=1, source_target_pairs={{1,0},{2,3},{5,4},{6,7},{9,8},{10,11},{13,12},{14,15},{16,17},{19,... | collective-permute-start | bytes 884744 | tf_op jit(solution)/shard_map/oq/ppermute | solution.py:318
  103.2 7.7 %collective-permute-start.23 = (bf16[128,512]{1,0:T(8,128)(2,1)S(1)}, bf16[128,512]{1,0:T(8,128)(2,1)S(1)}, u32[]{:S(2)}, u32[]{:S(2)}) collective-permute-start(bf16[128,512]{1,0:T(8,128)(2,1)S(1)} %get-tuple-element.84), channel_id=1, source_target_pairs={{0,2},{1,3},{2,4},{3,5},{4,6},{5,7},{6,0},{7,1},{8,10},{9,11},{10,... | collective-permute-start | bytes 393224 | tf_op jit(solution)/shard_map/up_st_right/ppermute | solution.py:318
  103.3 7.8 %collective-permute-start.24 = (bf16[128,512]{1,0:T(8,128)(2,1)S(1)}, bf16[128,512]{1,0:T(8,128)(2,1)S(1)}, u32[]{:S(2)}, u32[]{:S(2)}) collective-permute-start(bf16[128,512]{1,0:T(8,128)(2,1)S(1)} %get-tuple-element.85), channel_id=1, source_target_pairs={{0,6},{1,7},{2,0},{3,1},{4,2},{5,3},{6,4},{7,5},{8,14},{9,15},{10,... | collective-permute-start | bytes 393224 | tf_op jit(solution)/shard_map/down_st_right/ppermute | solution.py:318
  108.1 13.3 %collective-permute-start.22 = (bf16[128,640]{1,0:T(8,128)(2,1)S(1)}, bf16[128,640]{1,0:T(8,128)(2,1)S(1)}, u32[]{:S(2)}, u32[]{:S(2)}) collective-permute-start(bf16[128,640]{1,0:T(8,128)(2,1)S(1)} %get-tuple-element.82), channel_id=1, source_target_pairs={{0,1},{3,2},{4,5},{7,6},{8,9},{11,10},{12,13},{15,14},{17,16},{18,... | collective-permute-start | bytes 491528 | tf_op jit(solution)/shard_map/st/ppermute | solution.py:318
  113.0 8.4 %collective-permute-start.26 = (bf16[128,512]{1,0:T(8,128)(2,1)S(1)}, bf16[128,512]{1,0:T(8,128)(2,1)S(1)}, u32[]{:S(2)}, u32[]{:S(2)}) collective-permute-start(bf16[128,512]{1,0:T(8,128)(2,1)S(1)} %get-tuple-element.88), channel_id=1, source_target_pairs={{0,1},{3,2},{4,5},{7,6},{8,9},{11,10},{12,13},{15,14},{17,16},{18,... | collective-permute-start | bytes 393224 | tf_op jit(solution)/shard_map/st_right/ppermute | solution.py:318
  (7 other events, 24.3 us)

commit v3 on v2

--- a/solution.py
+++ b/solution.py
@@ -67,11 +67,14 @@
         value = value - parts[-1].astype(F32)
     return parts
 
+
 def dot(a, b):
     return lax.dot_general(a, b, (((1,), (0,)), ((), ())), preferred_element_type=F32)
 
-def condition_kernel(q, left, right, out, swapped, back, turned_left):
-    layers, count, width = q.shape
+
+def condition_kernel(q, left, right, out, back, turned_left):
+    count, layers = out.shape[0], q.shape[0]
+    width = q.shape[1] * q.shape[2] // count
     side = right.shape[1]
     four = 4 * side
     tiles = width // 128
@@ -83,26 +86,28 @@
     for l in range(layers):
         lanes = jnp.concatenate([right[l]] * 4, axis=1)
         wide_r = jnp.where(right_mask, jnp.concatenate([lanes] * 4, axis=0), 0.0)
-        x = q[l]
-        rows = jnp.concatenate([x[:, four * g : four * (g + 1)] for g in range(width // four)], axis=0)
-        first = sum(dot(rows, part) for part in reversed(thirds(wide_r)))
-        for g in range(width // four):
-            for h in range(four // 128):
-                swapped[g * (four // 128) + h] = first[count * g : count * (g + 1), 128 * h : 128 * (h + 1)]
-        half = side // 2
-        def halves(slot):
-            return [turned_left[slot, pl.ds(i, half, stride=2), :] for i in range(2)]
+        once = sum(dot(q[l], part) for part in reversed(thirds(wide_r)))
+        quarter = side // 4
+
+        def spread(slot, order):
+            return [turned_left[slot, pl.ds(i, quarter, stride=4), :] for i in order]
 
         turned_left[0] = jnp.concatenate([left[l]] * 2, axis=1)
-        low, high = halves(0)
+        low, high = (turned_left[0, pl.ds(i, side // 2, stride=2), :] for i in range(2))
         turn = jnp.concatenate([low] * 4 + [high] * 4, axis=0).T[:side]
         turned_left[1] = turn[:, :128]
         turned_left[2] = turn[:, 128:]
-        low, high = (jnp.concatenate(pair, axis=1) for pair in zip(halves(1), halves(2)))
+        rows = [jnp.concatenate(p, axis=1) for p in zip(spread(1, (0, 2, 1, 3)), spread(2, (0, 2, 1, 3)))]
+        low, high = jnp.concatenate(rows[:2], axis=0), jnp.concatenate(rows[2:], axis=0)
         wide_l = jnp.where(left_mask, jnp.concatenate([low] * 4 + [high] * 4, axis=0), 0.0)
         stack = []
+        groups = width // four
         for j in range(count // 4):
-            block = jnp.concatenate([swapped[:, 4 * j + i, :] for i in range(4)], axis=0).T
+            pieces = []
+            for i in range(4):
+                mine = once[groups * (4 * j + i) : groups * (4 * j + i + 1)]
+                pieces += [mine[:, :128], mine[:, 128:]]
+            block = jnp.concatenate(pieces, axis=0).T
             stack.append(jnp.concatenate([block[:side], block[side:]], axis=1))
         turned = thirds(jnp.concatenate(stack, axis=0))
         factor = thirds(wide_l)
@@ -121,9 +126,12 @@
             total = total + wide * wide
     out[:, layers * width :] = norm_columns(jnp.sum(total, axis=1, keepdims=True))
 
-def condition(q, left, right):
-    layers, count, width = q.shape
+
+def condition(queries, left, right):
+    count, layers, width = queries.shape
     side = left.shape[1]
+    four = 4 * side
+    q = jnp.transpose(queries.reshape(count, layers, width // four, four), (1, 0, 2, 3))
     vmem = pl.BlockSpec(memory_space=pltpu.VMEM)
     return pl.pallas_call(
         condition_kernel,
@@ -131,13 +139,12 @@
         in_specs=[vmem] * 3,
         out_specs=vmem,
         scratch_shapes=[
-            pltpu.VMEM((width // 128, count, 128), F32),
             pltpu.VMEM((count, width // 128, 128), F32),
             pltpu.VMEM((3, side, 128), F32),
         ],
         compiler_params=pltpu.CompilerParams(vmem_limit_bytes=24 * MIB),
         name="condition",
-    )(q, left, right)
+    )(q.reshape(layers, count * width // four, four), left, right)
 
 
 def fill(at, place, pieces, group):
@@ -347,7 +354,7 @@
     table = jnp.stack([jnp.asarray(v, jnp.int32) for t in tables for v in t])
     queries, table = lax.optimization_barrier((queries, table))
 
-    own = condition(jnp.swapaxes(queries, 0, 1), left_inverse, right_inverse)
+    own = condition(queries, left_inverse, right_inverse)
     s0 = send(own, SAME, "s0")
     q0 = send(own, OPPOSITE, "q0")
     o1 = send(own, ACROSS, "o1")

time: 123 us -> 123 us (level)
  Pallas kernels: 31.6 us -> 30.3 us
    optimization_barrier x1 -> x0, local copies, waits for them, and re-layouts: 1.81 us -> none  [per_device(): queries, table = lax.optimization_barrier((queries, table))]
    reshape x0 -> x2, local copies, waits for them, and re-layouts: none -> 1.81 us  [condition(): queries.reshape(count, layers, width // four, four)]
    pallas_call x1, Pallas kernels: 7.84 us -> 6.53 us  [condition(): pl.pallas_call(condition_kernel, out_shape=jax.ShapeDtypeStruct((count, l...]
where the time goes in v3:
time: 123 us; the launch traced here: 122 us
  waiting for transfers between devices  38.2 us (31%)
  starting transfers between devices  36.4 us (30%)
  Pallas kernels  30.3 us (25%)
  local copies, waits for them, and re-layouts  17.4 us (14%)
    ppermute x17, waiting for transfers between devices, send(): return lax.ppermute(value, 'rows', pairs)  26.1 us
    ppermute x12, starting transfers between devices, whole(): return lax.ppermute(value, BOTH, whole_perm(move))  23.2 us
    pallas_call x4, Pallas kernels, score_group(): pl.pallas_call(kernel, out_shape=out, in_specs=[pl.BlockSpec(memory_space...  21.4 us
    unnamed x5, local copies, waits for them, and re-layouts  15.5 us
    ppermute x17, starting transfers between devices, send(): return lax.ppermute(value, 'rows', pairs)  13.2 us
    ppermute x12, waiting for transfers between devices, whole(): return lax.ppermute(value, BOTH, whole_perm(move))  12.1 us
    pallas_call x1, Pallas kernels, condition(): pl.pallas_call(condition_kernel, out_shape=jax.ShapeDtypeStruct((count, l...  6.53 us
  transfers between devices with their start and end apart: 29, of which 10 were waited for; matrix products, arithmetic and copies ran while one was open for 12% of the time, Pallas kernels for 18%

profile of v3, /device:TPU:8, one launch (start us, length us, event | category | flops | bytes accessed | tf_op | source)
XLA Modules:
  0.0 122.4 jit_solution(15502584140451786969)
XLA Ops:
  0.1 1.7 %reshape.9 = bf16[64,2,16,256]{3,2,1,0:T(8,128)(2,1)S(1)} reshape(bf16[64,2,4096]{2,1,0:T(2,128)(2,1)} %param.4) | data formatting | bytes 2097152 | tf_op jit(solution)/shard_map/reshape | solution.py:134
  2.7 6.5 %condition.1.refs_0_ = bf16[64,8320]{1,0:T(8,128)(2,1)S(1)} custom-call(bf16[2,1024,256]{2,1,0:T(8,128)(2,1)S(1)} %bitcast.20, f32[2,64,64]{2,1,0:T(8,128)S(1)} %copy-done, f32[2,64,64]{2,1,0:T(8,128)S(1)} %copy-done.1), custom_call_target="tpu_custom_call" | custom-call | tf_op jit(solution)/shard_map/condition/pallas_call | solution.py:136
  9.6 2.5 %collective-permute-start.1 = (bf16[64,8320]{1,0:T(8,128)(2,1)S(1)}, bf16[64,8320]{1,0:T(8,128)(2,1)S(1)}, u32[]{:S(2)}, u32[]{:S(2)}) collective-permute-start(bf16[64,8320]{1,0:T(8,128)(2,1)S(1)} %condition.1.refs_0_), channel_id=1, source_target_pairs={{0,48},{8,56},{16,32},{24,40},{32,16},{40,24},{48,0},{56,8},{64,11... | collective-permute-start | bytes 3194888 | tf_op jit(solution)/shard_map/q0/ppermute | solution.py:321
  12.1 1.9 %collective-permute-start.2 = (bf16[64,8320]{1,0:T(8,128)(2,1)S(1)}, bf16[64,8320]{1,0:T(8,128)(2,1)S(1)}, u32[]{:S(2)}, u32[]{:S(2)}) collective-permute-start(bf16[64,8320]{1,0:T(8,128)(2,1)S(1)} %condition.1.refs_0_), channel_id=1, source_target_pairs={{0,64},{8,72},{16,80},{24,88},{32,96},{40,104},{48,112},{56,120},{... | collective-permute-start | bytes 3194888 | tf_op jit(solution)/shard_map/o1/ppermute | solution.py:321
  14.0 14.7 %copy.6 = bf16[128,8,2,4096]{3,1,2,0:T(8,128)(2,1)S(1)} copy(bf16[128,8,2,4096]{3,2,1,0:T(2,128)(2,1)} %bitcast.21) | data formatting | bytes 33554432
  28.7 5.8 %collective-permute-done.refs_0_ = bf16[64,8320]{1,0:T(8,128)(2,1)S(1)} collective-permute-done((bf16[64,8320]{1,0:T(8,128)(2,1)S(1)}, bf16[64,8320]{1,0:T(8,128)(2,1)S(1)}, u32[]{:S(2)}, u32[]{:S(2)}) %collective-permute-start) | collective-permute-done | bytes 1064992 | tf_op jit(solution)/shard_map/s0/ppermute | solution.py:321
  35.3 1.6 %collective-permute-done.2.refs_1_ = bf16[64,8320]{1,0:T(8,128)(2,1)S(1)} collective-permute-done((bf16[64,8320]{1,0:T(8,128)(2,1)S(1)}, bf16[64,8320]{1,0:T(8,128)(2,1)S(1)}, u32[]{:S(2)}, u32[]{:S(2)}) %collective-permute-start.2) | collective-permute-done | bytes 1064992 | tf_op jit(solution)/shard_map/o1/ppermute | solution.py:321
  37.3 2.4 %collective-permute-start.3 = (bf16[64,8320]{1,0:T(8,128)(2,1)S(1)}, bf16[64,8320]{1,0:T(8,128)(2,1)S(1)}, u32[]{:S(2)}, u32[]{:S(2)}) collective-permute-start(bf16[64,8320]{1,0:T(8,128)(2,1)S(1)} %collective-permute-done.1.refs_0_), channel_id=1, source_target_pairs={{0,16},{8,24},{16,0},{24,8},{32,48},{40,56},{48,32},{56,40},{64,80... | collective-permute-start | bytes 3194888 | tf_op jit(solution)/shard_map/t0/ppermute | solution.py:321
  39.7 1.9 %collective-permute-start.5 = (bf16[64,8320]{1,0:T(8,128)(2,1)S(1)}, bf16[64,8320]{1,0:T(8,128)(2,1)S(1)}, u32[]{:S(2)}, u32[]{:S(2)}) collective-permute-start(bf16[64,8320]{1,0:T(8,128)(2,1)S(1)} %collective-permute-done.refs_0_), channel_id=1, source_target_pairs={{0,64},{8,72},{16,80},{24,88},{32,96},{40,104},{48,112},{56,120},{... | collective-permute-start | bytes 3194888 | tf_op jit(solution)/shard_map/s1/ppermute | solution.py:321
  42.1 5.3 %score_group.2.refs_5_ = bf16[256,1152]{1,0:T(8,128)(2,1)S(1)} custom-call(s32[15]{0:T(128)S(1)} %stack.55.place.which, bf16[64,8320]{1,0:T(8,128)(2,1)S(1)} %condition.1.refs_0_, bf16[64,8320]{1,0:T(8,128)(2,1)S(1)} %collective-permute-done.2.refs_1_, bf16[64,8320]{1,0:T(8,128)(2,1)S(1)} %collective-permute-done.6.refs_2_, ...), custom_call_target="tpu_custom_call" | custom-call | flops 4294967296 | bytes 16777216 | tf_op jit(solution)/shard_map/score_group/pallas_call | solution.py:210
  47.4 16.2 %collective-permute-done.3.b.refs_0_ = bf16[64,8320]{1,0:T(8,128)(2,1)S(1)} collective-permute-done((bf16[64,8320]{1,0:T(8,128)(2,1)S(1)}, bf16[64,8320]{1,0:T(8,128)(2,1)S(1)}, u32[]{:S(2)}, u32[]{:S(2)}) %collective-permute-start.3) | collective-permute-done | bytes 1064992 | tf_op jit(solution)/shard_map/t0/ppermute | solution.py:321
  63.6 1.6 %collective-permute-done.5.refs_1_ = bf16[64,8320]{1,0:T(8,128)(2,1)S(1)} collective-permute-done((bf16[64,8320]{1,0:T(8,128)(2,1)S(1)}, bf16[64,8320]{1,0:T(8,128)(2,1)S(1)}, u32[]{:S(2)}, u32[]{:S(2)}) %collective-permute-start.5) | collective-permute-done | bytes 1064992 | tf_op jit(solution)/shard_map/s1/ppermute | solution.py:321
  65.8 1.8 %collective-permute-start.10 = (bf16[32,8320]{1,0:T(8,128)(2,1)S(1)}, bf16[32,8320]{1,0:T(8,128)(2,1)S(1)}, u32[]{:S(2)}, u32[]{:S(2)}) collective-permute-start(bf16[32,8320]{1,0:T(8,128)(2,1)S(1)} %get-tuple-element.59), channel_id=1, source_target_pairs={{0,64},{8,72},{16,80},{24,88},{32,96},{40,104},{48,112},{56,120},{... | collective-permute-start | bytes 1597448 | tf_op jit(solution)/shard_map/t1b/ppermute | solution.py:321
  68.1 5.4 %score_and_deal.2 = (bf16[128,1152]{1,0:T(8,128)(2,1)S(1)}, bf16[128,1152]{1,0:T(8,128)(2,1)S(1)}, bf16[128,1152]{1,0:T(8,128)(2,1)S(1)}, bf16[128,1152]{1,0:T(8,128)(2,1)S(1)}) custom-call(s32[15]{0:T(128)S(1)} %stack.55.place.which, bf16[64,8320]{1,0:T(8,128)(2,1)S(1)} %collective-permute-done.1.refs_0_, ...), custom_call_target="tpu_custom_call" | custom-call | flops 4294967296 | bytes 16777216 | tf_op jit(solution)/shard_map/score_and_deal/pallas_call | solution.py:210
  73.5 1.6 %collective-permute-start.15 = (bf16[128,1152]{1,0:T(8,128)(2,1)S(1)}, bf16[128,1152]{1,0:T(8,128)(2,1)S(1)}, u32[]{:S(2)}, u32[]{:S(2)}) collective-permute-start(bf16[128,1152]{1,0:T(8,128)(2,1)S(1)} %get-tuple-element.67), channel_id=1, source_target_pairs={{0,2},{1,3},{2,4},{3,5},{4,6},{5,7},{6,0},{7,1},{8,10},{9,11},{10,... | collective-permute-start | bytes 884744 | tf_op jit(solution)/shard_map/up_oq/ppermute | solution.py:325
  75.1 1.7 %collective-permute-start.16 = (bf16[128,1152]{1,0:T(8,128)(2,1)S(1)}, bf16[128,1152]{1,0:T(8,128)(2,1)S(1)}, u32[]{:S(2)}, u32[]{:S(2)}) collective-permute-start(bf16[128,1152]{1,0:T(8,128)(2,1)S(1)} %get-tuple-element.69), channel_id=1, source_target_pairs={{0,6},{1,7},{2,0},{3,1},{4,2},{5,3},{6,4},{7,5},{8,14},{9,15},{10,... | collective-permute-start | bytes 884744 | tf_op jit(solution)/shard_map/down_oq/ppermute | solution.py:325
  76.8 5.3 %score_group.3.refs_7_ = bf16[256,1152]{1,0:T(8,128)(2,1)S(1)} custom-call(s32[15]{0:T(128)S(1)} %stack.55.place.which, bf16[64,8320]{1,0:T(8,128)(2,1)S(1)} %collective-permute-done.refs_0_, bf16[64,8320]{1,0:T(8,128)(2,1)S(1)} %collective-permute-done.5.refs_1_, bf16[64,8320]{1,0:T(8,128)(2,1)S(1)} %collective-permute-done.8.refs_2_, ...), custom_call_target="tpu_custom_call" | custom-call | flops 4294967296 | bytes 16777216 | tf_op jit(solution)/shard_map/score_group/pallas_call | solution.py:210
  84.2 2.7 %collective-permute-start.27 = (bf16[128,1152]{1,0:T(8,128)(2,1)S(1)}, bf16[128,1152]{1,0:T(8,128)(2,1)S(1)}, u32[]{:S(2)}, u32[]{:S(2)}) collective-permute-start(bf16[128,1152]{1,0:T(8,128)(2,1)S(1)} %get-tuple-element.68), channel_id=1, source_target_pairs={{0,4},{1,5},{2,6},{3,7},{4,0},{5,1},{6,2},{7,3},{8,12},{9,13},{10,... | collective-permute-start | bytes 884744 | tf_op jit(solution)/shard_map/over_oq/ppermute | solution.py:325
  86.9 5.4 %score_and_deal.3 = (bf16[128,640]{1,0:T(8,128)(2,1)S(1)}, bf16[128,512]{1,0:T(8,128)(2,1)S(1)}, bf16[128,640]{1,0:T(8,128)(2,1)S(1)}, bf16[128,512]{1,0:T(8,128...) custom-call(s32[15]{0:T(128)S(1)} %stack.55.place.which, ...), custom_call_target="tpu_custom_call" | custom-call | flops 4294967296 | bytes 16777216 | tf_op jit(solution)/shard_map/score_and_deal/pallas_call | solution.py:210
  93.6 2.0 %collective-permute-start.20 = (bf16[128,640]{1,0:T(8,128)(2,1)S(1)}, bf16[128,640]{1,0:T(8,128)(2,1)S(1)}, u32[]{:S(2)}, u32[]{:S(2)}) collective-permute-start(bf16[128,640]{1,0:T(8,128)(2,1)S(1)} %get-tuple-element.79), channel_id=1, source_target_pairs={{0,6},{1,7},{2,0},{3,1},{4,2},{5,3},{6,4},{7,5},{8,14},{9,15},{10,... | collective-permute-start | bytes 491528 | tf_op jit(solution)/shard_map/down_st/ppermute | solution.py:325
  97.0 5.6 %collective-permute-start.28 = (bf16[128,1152]{1,0:T(8,128)(2,1)S(1)}, bf16[128,1152]{1,0:T(8,128)(2,1)S(1)}, u32[]{:S(2)}, u32[]{:S(2)}) collective-permute-start(bf16[128,1152]{1,0:T(8,128)(2,1)S(1)} %get-tuple-element.92), channel_id=1, source_target_pairs={{1,0},{2,3},{5,4},{6,7},{9,8},{10,11},{13,12},{14,15},{16,17},{19,... | collective-permute-start | bytes 884744 | tf_op jit(solution)/shard_map/oq/ppermute | solution.py:325
  102.7 3.2 %collective-permute-start.24 = (bf16[128,512]{1,0:T(8,128)(2,1)S(1)}, bf16[128,512]{1,0:T(8,128)(2,1)S(1)}, u32[]{:S(2)}, u32[]{:S(2)}) collective-permute-start(bf16[128,512]{1,0:T(8,128)(2,1)S(1)} %get-tuple-element.85), channel_id=1, source_target_pairs={{0,6},{1,7},{2,0},{3,1},{4,2},{5,3},{6,4},{7,5},{8,14},{9,15},{10,... | collective-permute-start | bytes 393224 | tf_op jit(solution)/shard_map/down_st_right/ppermute | solution.py:325
  110.5 1.9 %collective-permute-done.25.c = bf16[128,512]{1,0:T(8,128)(2,1)S(1)} collective-permute-done((bf16[128,512]{1,0:T(8,128)(2,1)S(1)}, bf16[128,512]{1,0:T(8,128)(2,1)S(1)}, u32[]{:S(2)}, u32[]{:S(2)}) %collective-permute-start.25) | collective-permute-done | bytes 131104 | tf_op jit(solution)/shard_map/over_st_right/ppermute | solution.py:325
  113.8 7.1 %collective-permute-done.26.refs_3_ = bf16[128,512]{1,0:T(8,128)(2,1)S(1)} collective-permute-done((bf16[128,512]{1,0:T(8,128)(2,1)S(1)}, bf16[128,512]{1,0:T(8,128)(2,1)S(1)}, u32[]{:S(2)}, u32[]{:S(2)}) %collective-permute-start.26) | collective-permute-done | bytes 131104 | tf_op jit(solution)/shard_map/st_right/ppermute | solution.py:325
  (52 shorter events, 16.2 us)
Async XLA Ops:
  9.2 25.3 %collective-permute-start = (bf16[64,8320]{1,0:T(8,128)(2,1)S(1)}, bf16[64,8320]{1,0:T(8,128)(2,1)S(1)}, u32[]{:S(2)}, u32[]{:S(2)}) collective-permute-start(bf16[64,8320]{1,0:T(8,128)(2,1)S(1)} %condition.1.refs_0_), channel_id=1, source_target_pairs={{0,16},{8,24},{16,0},{24,8},{32,48},{40,56},{48,32},{56,40},{64,80... | collective-permute-start | bytes 3194888 | tf_op jit(solution)/shard_map/s0/ppermute | solution.py:321
  9.6 25.7 %collective-permute-start.1 = (bf16[64,8320]{1,0:T(8,128)(2,1)S(1)}, bf16[64,8320]{1,0:T(8,128)(2,1)S(1)}, u32[]{:S(2)}, u32[]{:S(2)}) collective-permute-start(bf16[64,8320]{1,0:T(8,128)(2,1)S(1)} %condition.1.refs_0_), channel_id=1, source_target_pairs={{0,48},{8,56},{16,32},{24,40},{32,16},{40,24},{48,0},{56,8},{64,11... | collective-permute-start | bytes 3194888 | tf_op jit(solution)/shard_map/q0/ppermute | solution.py:321
  12.1 24.9 %collective-permute-start.2 = (bf16[64,8320]{1,0:T(8,128)(2,1)S(1)}, bf16[64,8320]{1,0:T(8,128)(2,1)S(1)}, u32[]{:S(2)}, u32[]{:S(2)}) collective-permute-start(bf16[64,8320]{1,0:T(8,128)(2,1)S(1)} %condition.1.refs_0_), channel_id=1, source_target_pairs={{0,64},{8,72},{16,80},{24,88},{32,96},{40,104},{48,112},{56,120},{... | collective-permute-start | bytes 3194888 | tf_op jit(solution)/shard_map/o1/ppermute | solution.py:321
  14.0 27.5 %collective-permute-start.6 = (bf16[64,8320]{1,0:T(8,128)(2,1)S(1)}, bf16[64,8320]{1,0:T(8,128)(2,1)S(1)}, u32[]{:S(2)}, u32[]{:S(2)}) collective-permute-start(bf16[64,8320]{1,0:T(8,128)(2,1)S(1)} %condition.1.refs_0_), channel_id=1, source_target_pairs={{0,8},{8,0},{16,24},{24,16},{32,40},{40,32},{48,56},{56,48},{64,72... | collective-permute-start | bytes 3194888 | tf_op jit(solution)/shard_map/own_sib/ppermute | solution.py:321
  37.0 26.6 %collective-permute-start.4 = (bf16[64,8320]{1,0:T(8,128)(2,1)S(1)}, bf16[64,8320]{1,0:T(8,128)(2,1)S(1)}, u32[]{:S(2)}, u32[]{:S(2)}) collective-permute-start(bf16[64,8320]{1,0:T(8,128)(2,1)S(1)} %collective-permute-done.2.refs_1_), channel_id=1, source_target_pairs={{0,48},{8,56},{16,32},{24,40},{32,16},{40,24},{48,0},{56,8},{64,11... | collective-permute-start | bytes 3194888 | tf_op jit(solution)/shard_map/q1/ppermute | solution.py:321
  37.3 26.3 %collective-permute-start.3 = (bf16[64,8320]{1,0:T(8,128)(2,1)S(1)}, bf16[64,8320]{1,0:T(8,128)(2,1)S(1)}, u32[]{:S(2)}, u32[]{:S(2)}) collective-permute-start(bf16[64,8320]{1,0:T(8,128)(2,1)S(1)} %collective-permute-done.1.refs_0_), channel_id=1, source_target_pairs={{0,16},{8,24},{16,0},{24,8},{32,48},{40,56},{48,32},{56,40},{64,80... | collective-permute-start | bytes 3194888 | tf_op jit(solution)/shard_map/t0/ppermute | solution.py:321
  39.7 25.5 %collective-permute-start.5 = (bf16[64,8320]{1,0:T(8,128)(2,1)S(1)}, bf16[64,8320]{1,0:T(8,128)(2,1)S(1)}, u32[]{:S(2)}, u32[]{:S(2)}) collective-permute-start(bf16[64,8320]{1,0:T(8,128)(2,1)S(1)} %collective-permute-done.refs_0_), channel_id=1, source_target_pairs={{0,64},{8,72},{16,80},{24,88},{32,96},{40,104},{48,112},{56,120},{... | collective-permute-start | bytes 3194888 | tf_op jit(solution)/shard_map/s1/ppermute | solution.py:321
  41.6 23.6 %collective-permute-start.8 = (bf16[64,8320]{1,0:T(8,128)(2,1)S(1)}, bf16[64,8320]{1,0:T(8,128)(2,1)S(1)}, u32[]{:S(2)}, u32[]{:S(2)}) collective-permute-start(bf16[64,8320]{1,0:T(8,128)(2,1)S(1)} %collective-permute-done.refs_0_), channel_id=1, source_target_pairs={{0,8},{8,0},{16,24},{24,16},{32,40},{40,32},{48,56},{56,48},{64,72... | collective-permute-start | bytes 3194888 | tf_op jit(solution)/shard_map/s0_sib/ppermute | solution.py:321
  41.6 26.0 %collective-permute-start.11 = (bf16[64,8320]{1,0:T(8,128)(2,1)S(1)}, bf16[64,8320]{1,0:T(8,128)(2,1)S(1)}, u32[]{:S(2)}, u32[]{:S(2)}) collective-permute-start(bf16[64,8320]{1,0:T(8,128)(2,1)S(1)} %collective-permute-done.1.refs_0_), channel_id=1, source_target_pairs={{0,8},{8,0},{16,24},{24,16},{32,40},{40,32},{48,56},{56,48},{64,72... | collective-permute-start | bytes 3194888 | tf_op jit(solution)/shard_map/q0_sib/ppermute | solution.py:321
  65.2 8.3 %collective-permute-start.13 = (bf16[64,8320]{1,0:T(8,128)(2,1)S(1)}, bf16[64,8320]{1,0:T(8,128)(2,1)S(1)}, u32[]{:S(2)}, u32[]{:S(2)}) collective-permute-start(bf16[64,8320]{1,0:T(8,128)(2,1)S(1)} %collective-permute-done.5.refs_1_), channel_id=1, source_target_pairs={{0,8},{8,0},{16,24},{24,16},{32,40},{40,32},{48,56},{56,48},{64,72... | collective-permute-start | bytes 3194888 | tf_op jit(solution)/shard_map/s1_sib/ppermute | solution.py:321
  65.7 7.8 %collective-permute-start.14 = (bf16[64,8320]{1,0:T(8,128)(2,1)S(1)}, bf16[64,8320]{1,0:T(8,128)(2,1)S(1)}, u32[]{:S(2)}, u32[]{:S(2)}) collective-permute-start(bf16[64,8320]{1,0:T(8,128)(2,1)S(1)} %collective-permute-done.3.b.refs_0_), channel_id=1, source_target_pairs={{0,8},{8,0},{16,24},{24,16},{32,40},{40,32},{48,56},{56,48},{64,72... | collective-permute-start | bytes 3194888 | tf_op jit(solution)/shard_map/t0_sib/ppermute | solution.py:321
  65.8 16.3 %collective-permute-start.10 = (bf16[32,8320]{1,0:T(8,128)(2,1)S(1)}, bf16[32,8320]{1,0:T(8,128)(2,1)S(1)}, u32[]{:S(2)}, u32[]{:S(2)}) collective-permute-start(bf16[32,8320]{1,0:T(8,128)(2,1)S(1)} %get-tuple-element.59), channel_id=1, source_target_pairs={{0,64},{8,72},{16,80},{24,88},{32,96},{40,104},{48,112},{56,120},{... | collective-permute-start | bytes 1597448 | tf_op jit(solution)/shard_map/t1b/ppermute | solution.py:321
  67.6 14.5 %collective-permute-start.9 = (bf16[32,8320]{1,0:T(8,128)(2,1)S(1)}, bf16[32,8320]{1,0:T(8,128)(2,1)S(1)}, u32[]{:S(2)}, u32[]{:S(2)}) collective-permute-start(bf16[32,8320]{1,0:T(8,128)(2,1)S(1)} %get-tuple-element.58), channel_id=1, source_target_pairs={{0,16},{8,24},{16,0},{24,8},{32,48},{40,56},{48,32},{56,40},{64,80... | collective-permute-start | bytes 1597448 | tf_op jit(solution)/shard_map/t1a/ppermute | solution.py:321
  73.5 10.1 %collective-permute-start.15 = (bf16[128,1152]{1,0:T(8,128)(2,1)S(1)}, bf16[128,1152]{1,0:T(8,128)(2,1)S(1)}, u32[]{:S(2)}, u32[]{:S(2)}) collective-permute-start(bf16[128,1152]{1,0:T(8,128)(2,1)S(1)} %get-tuple-element.67), channel_id=1, source_target_pairs={{0,2},{1,3},{2,4},{3,5},{4,6},{5,7},{6,0},{7,1},{8,10},{9,11},{10,... | collective-permute-start | bytes 884744 | tf_op jit(solution)/shard_map/up_oq/ppermute | solution.py:325
  75.1 8.6 %collective-permute-start.16 = (bf16[128,1152]{1,0:T(8,128)(2,1)S(1)}, bf16[128,1152]{1,0:T(8,128)(2,1)S(1)}, u32[]{:S(2)}, u32[]{:S(2)}) collective-permute-start(bf16[128,1152]{1,0:T(8,128)(2,1)S(1)} %get-tuple-element.69), channel_id=1, source_target_pairs={{0,6},{1,7},{2,0},{3,1},{4,2},{5,3},{6,4},{7,5},{8,14},{9,15},{10,... | collective-permute-start | bytes 884744 | tf_op jit(solution)/shard_map/down_oq/ppermute | solution.py:325
  84.2 12.4 %collective-permute-start.27 = (bf16[128,1152]{1,0:T(8,128)(2,1)S(1)}, bf16[128,1152]{1,0:T(8,128)(2,1)S(1)}, u32[]{:S(2)}, u32[]{:S(2)}) collective-permute-start(bf16[128,1152]{1,0:T(8,128)(2,1)S(1)} %get-tuple-element.68), channel_id=1, source_target_pairs={{0,4},{1,5},{2,6},{3,7},{4,0},{5,1},{6,2},{7,3},{8,12},{9,13},{10,... | collective-permute-start | bytes 884744 | tf_op jit(solution)/shard_map/over_oq/ppermute | solution.py:325
  92.3 10.4 %collective-permute-start.19 = (bf16[128,640]{1,0:T(8,128)(2,1)S(1)}, bf16[128,640]{1,0:T(8,128)(2,1)S(1)}, u32[]{:S(2)}, u32[]{:S(2)}) collective-permute-start(bf16[128,640]{1,0:T(8,128)(2,1)S(1)} %get-tuple-element.78), channel_id=1, source_target_pairs={{0,2},{1,3},{2,4},{3,5},{4,6},{5,7},{6,0},{7,1},{8,10},{9,11},{10,... | collective-permute-start | bytes 491528 | tf_op jit(solution)/shard_map/up_st/ppermute | solution.py:325
  93.6 12.4 %collective-permute-start.20 = (bf16[128,640]{1,0:T(8,128)(2,1)S(1)}, bf16[128,640]{1,0:T(8,128)(2,1)S(1)}, u32[]{:S(2)}, u32[]{:S(2)}) collective-permute-start(bf16[128,640]{1,0:T(8,128)(2,1)S(1)} %get-tuple-element.79), channel_id=1, source_target_pairs={{0,6},{1,7},{2,0},{3,1},{4,2},{5,3},{6,4},{7,5},{8,14},{9,15},{10,... | collective-permute-start | bytes 491528 | tf_op jit(solution)/shard_map/down_st/ppermute | solution.py:325
  95.7 11.7 %collective-permute-start.21 = (bf16[128,640]{1,0:T(8,128)(2,1)S(1)}, bf16[128,640]{1,0:T(8,128)(2,1)S(1)}, u32[]{:S(2)}, u32[]{:S(2)}) collective-permute-start(bf16[128,640]{1,0:T(8,128)(2,1)S(1)} %get-tuple-element.80), channel_id=1, source_target_pairs={{0,4},{1,5},{2,6},{3,7},{4,0},{5,1},{6,2},{7,3},{8,12},{9,13},{10,... | collective-permute-start | bytes 491528 | tf_op jit(solution)/shard_map/over_st/ppermute | solution.py:325
  97.0 16.8 %collective-permute-start.28 = (bf16[128,1152]{1,0:T(8,128)(2,1)S(1)}, bf16[128,1152]{1,0:T(8,128)(2,1)S(1)}, u32[]{:S(2)}, u32[]{:S(2)}) collective-permute-start(bf16[128,1152]{1,0:T(8,128)(2,1)S(1)} %get-tuple-element.92), channel_id=1, source_target_pairs={{1,0},{2,3},{5,4},{6,7},{9,8},{10,11},{13,12},{14,15},{16,17},{19,... | collective-permute-start | bytes 884744 | tf_op jit(solution)/shard_map/oq/ppermute | solution.py:325
  102.6 7.7 %collective-permute-start.23 = (bf16[128,512]{1,0:T(8,128)(2,1)S(1)}, bf16[128,512]{1,0:T(8,128)(2,1)S(1)}, u32[]{:S(2)}, u32[]{:S(2)}) collective-permute-start(bf16[128,512]{1,0:T(8,128)(2,1)S(1)} %get-tuple-element.84), channel_id=1, source_target_pairs={{0,2},{1,3},{2,4},{3,5},{4,6},{5,7},{6,0},{7,1},{8,10},{9,11},{10,... | collective-permute-start | bytes 393224 | tf_op jit(solution)/shard_map/up_st_right/ppermute | solution.py:325
  102.7 7.8 %collective-permute-start.24 = (bf16[128,512]{1,0:T(8,128)(2,1)S(1)}, bf16[128,512]{1,0:T(8,128)(2,1)S(1)}, u32[]{:S(2)}, u32[]{:S(2)}) collective-permute-start(bf16[128,512]{1,0:T(8,128)(2,1)S(1)} %get-tuple-element.85), channel_id=1, source_target_pairs={{0,6},{1,7},{2,0},{3,1},{4,2},{5,3},{6,4},{7,5},{8,14},{9,15},{10,... | collective-permute-start | bytes 393224 | tf_op jit(solution)/shard_map/down_st_right/ppermute | solution.py:325
  107.6 13.3 %collective-permute-start.22 = (bf16[128,640]{1,0:T(8,128)(2,1)S(1)}, bf16[128,640]{1,0:T(8,128)(2,1)S(1)}, u32[]{:S(2)}, u32[]{:S(2)}) collective-permute-start(bf16[128,640]{1,0:T(8,128)(2,1)S(1)} %get-tuple-element.82), channel_id=1, source_target_pairs={{0,1},{3,2},{4,5},{7,6},{8,9},{11,10},{12,13},{15,14},{17,16},{18,... | collective-permute-start | bytes 491528 | tf_op jit(solution)/shard_map/st/ppermute | solution.py:325
  112.5 8.4 %collective-permute-start.26 = (bf16[128,512]{1,0:T(8,128)(2,1)S(1)}, bf16[128,512]{1,0:T(8,128)(2,1)S(1)}, u32[]{:S(2)}, u32[]{:S(2)}) collective-permute-start(bf16[128,512]{1,0:T(8,128)(2,1)S(1)} %get-tuple-element.88), channel_id=1, source_target_pairs={{0,1},{3,2},{4,5},{7,6},{8,9},{11,10},{12,13},{15,14},{17,16},{18,... | collective-permute-start | bytes 393224 | tf_op jit(solution)/shard_map/st_right/ppermute | solution.py:325
  (7 other events, 22.1 us)

commit v4 on v3

--- a/solution.py
+++ b/solution.py
@@ -86,7 +86,7 @@
     for l in range(layers):
         lanes = jnp.concatenate([right[l]] * 4, axis=1)
         wide_r = jnp.where(right_mask, jnp.concatenate([lanes] * 4, axis=0), 0.0)
-        once = sum(dot(q[l], part) for part in reversed(thirds(wide_r)))
+        once = dot(jnp.concatenate([q[l]] * 3, axis=1), jnp.concatenate(thirds(wide_r)[::-1], axis=0))
         quarter = side // 4
 
         def spread(slot, order):
@@ -111,9 +111,11 @@
             stack.append(jnp.concatenate([block[:side], block[side:]], axis=1))
         turned = thirds(jnp.concatenate(stack, axis=0))
         factor = thirds(wide_l)
-        second = dot(turned[1], factor[1]) + dot(turned[0], factor[2]) + dot(turned[2], factor[0])
-        second = second + (dot(turned[0], factor[1]) + dot(turned[1], factor[0]))
-        second = second + dot(turned[0], factor[0])
+        terms = ((1, 1), (0, 2), (2, 0), (0, 1), (1, 0), (0, 0))
+        second = dot(
+            jnp.concatenate([turned[i] for i, _ in terms], axis=1),
+            jnp.concatenate([factor[k] for _, k in terms], axis=0),
+        )
         for j in range(count // 4):
             piece = second[side * j : side * (j + 1)]
             block = jnp.concatenate([piece[:, :128], piece[:, 128:]], axis=0).T

time: 123 us -> 123 us (level)
  no operation moved by 1% of the time
where the time goes in v4:
time: 123 us; the launch traced here: 122 us
  waiting for transfers between devices  38.2 us (31%)
  starting transfers between devices  36.4 us (30%)
  Pallas kernels  30.3 us (25%)
  local copies, waits for them, and re-layouts  17.4 us (14%)
    ppermute x17, waiting for transfers between devices, send(): return lax.ppermute(value, 'rows', pairs)  26.1 us
    ppermute x12, starting transfers between devices, whole(): return lax.ppermute(value, BOTH, whole_perm(move))  23.2 us
    pallas_call x4, Pallas kernels, score_group(): pl.pallas_call(kernel, out_shape=out, in_specs=[pl.BlockSpec(memory_space...  21.4 us
    unnamed x5, local copies, waits for them, and re-layouts  15.5 us
    ppermute x17, starting transfers between devices, send(): return lax.ppermute(value, 'rows', pairs)  13.2 us
    ppermute x12, waiting for transfers between devices, whole(): return lax.ppermute(value, BOTH, whole_perm(move))  12.1 us
    pallas_call x1, Pallas kernels, condition(): pl.pallas_call(condition_kernel, out_shape=jax.ShapeDtypeStruct((count, l...  6.57 us
  transfers between devices with their start and end apart: 29, of which 10 were waited for; matrix products, arithmetic and copies ran while one was open for 12% of the time, Pallas kernels for 18%

profile of v4, /device:TPU:8, one launch (start us, length us, event | category | flops | bytes accessed | tf_op | source)
XLA Modules:
  0.0 122.4 jit_solution(7074747304923741036)
XLA Ops:
  0.1 1.7 %reshape.9 = bf16[64,2,16,256]{3,2,1,0:T(8,128)(2,1)S(1)} reshape(bf16[64,2,4096]{2,1,0:T(2,128)(2,1)} %param.4) | data formatting | bytes 2097152 | tf_op jit(solution)/shard_map/reshape | solution.py:136
  2.7 6.6 %condition.1.refs_0_ = bf16[64,8320]{1,0:T(8,128)(2,1)S(1)} custom-call(bf16[2,1024,256]{2,1,0:T(8,128)(2,1)S(1)} %bitcast.20, f32[2,64,64]{2,1,0:T(8,128)S(1)} %copy-done, f32[2,64,64]{2,1,0:T(8,128)S(1)} %copy-done.1), custom_call_target="tpu_custom_call" | custom-call | tf_op jit(solution)/shard_map/condition/pallas_call | solution.py:138
  9.7 2.5 %collective-permute-start.1 = (bf16[64,8320]{1,0:T(8,128)(2,1)S(1)}, bf16[64,8320]{1,0:T(8,128)(2,1)S(1)}, u32[]{:S(2)}, u32[]{:S(2)}) collective-permute-start(bf16[64,8320]{1,0:T(8,128)(2,1)S(1)} %condition.1.refs_0_), channel_id=1, source_target_pairs={{0,48},{8,56},{16,32},{24,40},{32,16},{40,24},{48,0},{56,8},{64,11... | collective-permute-start | bytes 3194888 | tf_op jit(solution)/shard_map/q0/ppermute | solution.py:323
  12.2 1.9 %collective-permute-start.2 = (bf16[64,8320]{1,0:T(8,128)(2,1)S(1)}, bf16[64,8320]{1,0:T(8,128)(2,1)S(1)}, u32[]{:S(2)}, u32[]{:S(2)}) collective-permute-start(bf16[64,8320]{1,0:T(8,128)(2,1)S(1)} %condition.1.refs_0_), channel_id=1, source_target_pairs={{0,64},{8,72},{16,80},{24,88},{32,96},{40,104},{48,112},{56,120},{... | collective-permute-start | bytes 3194888 | tf_op jit(solution)/shard_map/o1/ppermute | solution.py:323
  14.1 14.7 %copy.6 = bf16[128,8,2,4096]{3,1,2,0:T(8,128)(2,1)S(1)} copy(bf16[128,8,2,4096]{3,2,1,0:T(2,128)(2,1)} %bitcast.21) | data formatting | bytes 33554432
  28.8 5.8 %collective-permute-done.refs_0_ = bf16[64,8320]{1,0:T(8,128)(2,1)S(1)} collective-permute-done((bf16[64,8320]{1,0:T(8,128)(2,1)S(1)}, bf16[64,8320]{1,0:T(8,128)(2,1)S(1)}, u32[]{:S(2)}, u32[]{:S(2)}) %collective-permute-start) | collective-permute-done | bytes 1064992 | tf_op jit(solution)/shard_map/s0/ppermute | solution.py:323
  35.4 1.6 %collective-permute-done.2.refs_1_ = bf16[64,8320]{1,0:T(8,128)(2,1)S(1)} collective-permute-done((bf16[64,8320]{1,0:T(8,128)(2,1)S(1)}, bf16[64,8320]{1,0:T(8,128)(2,1)S(1)}, u32[]{:S(2)}, u32[]{:S(2)}) %collective-permute-start.2) | collective-permute-done | bytes 1064992 | tf_op jit(solution)/shard_map/o1/ppermute | solution.py:323
  37.3 2.4 %collective-permute-start.3 = (bf16[64,8320]{1,0:T(8,128)(2,1)S(1)}, bf16[64,8320]{1,0:T(8,128)(2,1)S(1)}, u32[]{:S(2)}, u32[]{:S(2)}) collective-permute-start(bf16[64,8320]{1,0:T(8,128)(2,1)S(1)} %collective-permute-done.1.refs_0_), channel_id=1, source_target_pairs={{0,16},{8,24},{16,0},{24,8},{32,48},{40,56},{48,32},{56,40},{64,80... | collective-permute-start | bytes 3194888 | tf_op jit(solution)/shard_map/t0/ppermute | solution.py:323
  39.7 1.9 %collective-permute-start.5 = (bf16[64,8320]{1,0:T(8,128)(2,1)S(1)}, bf16[64,8320]{1,0:T(8,128)(2,1)S(1)}, u32[]{:S(2)}, u32[]{:S(2)}) collective-permute-start(bf16[64,8320]{1,0:T(8,128)(2,1)S(1)} %collective-permute-done.refs_0_), channel_id=1, source_target_pairs={{0,64},{8,72},{16,80},{24,88},{32,96},{40,104},{48,112},{56,120},{... | collective-permute-start | bytes 3194888 | tf_op jit(solution)/shard_map/s1/ppermute | solution.py:323
  42.1 5.3 %score_group.2.refs_5_ = bf16[256,1152]{1,0:T(8,128)(2,1)S(1)} custom-call(s32[15]{0:T(128)S(1)} %stack.55.place.which, bf16[64,8320]{1,0:T(8,128)(2,1)S(1)} %condition.1.refs_0_, bf16[64,8320]{1,0:T(8,128)(2,1)S(1)} %collective-permute-done.2.refs_1_, bf16[64,8320]{1,0:T(8,128)(2,1)S(1)} %collective-permute-done.6.refs_2_, ...), custom_call_target="tpu_custom_call" | custom-call | flops 4294967296 | bytes 16777216 | tf_op jit(solution)/shard_map/score_group/pallas_call | solution.py:212
  47.4 16.2 %collective-permute-done.3.b.refs_0_ = bf16[64,8320]{1,0:T(8,128)(2,1)S(1)} collective-permute-done((bf16[64,8320]{1,0:T(8,128)(2,1)S(1)}, bf16[64,8320]{1,0:T(8,128)(2,1)S(1)}, u32[]{:S(2)}, u32[]{:S(2)}) %collective-permute-start.3) | collective-permute-done | bytes 1064992 | tf_op jit(solution)/shard_map/t0/ppermute | solution.py:323
  63.6 1.6 %collective-permute-done.5.refs_1_ = bf16[64,8320]{1,0:T(8,128)(2,1)S(1)} collective-permute-done((bf16[64,8320]{1,0:T(8,128)(2,1)S(1)}, bf16[64,8320]{1,0:T(8,128)(2,1)S(1)}, u32[]{:S(2)}, u32[]{:S(2)}) %collective-permute-start.5) | collective-permute-done | bytes 1064992 | tf_op jit(solution)/shard_map/s1/ppermute | solution.py:323
  65.8 1.8 %collective-permute-start.10 = (bf16[32,8320]{1,0:T(8,128)(2,1)S(1)}, bf16[32,8320]{1,0:T(8,128)(2,1)S(1)}, u32[]{:S(2)}, u32[]{:S(2)}) collective-permute-start(bf16[32,8320]{1,0:T(8,128)(2,1)S(1)} %get-tuple-element.59), channel_id=1, source_target_pairs={{0,64},{8,72},{16,80},{24,88},{32,96},{40,104},{48,112},{56,120},{... | collective-permute-start | bytes 1597448 | tf_op jit(solution)/shard_map/t1b/ppermute | solution.py:323
  68.1 5.4 %score_and_deal.2 = (bf16[128,1152]{1,0:T(8,128)(2,1)S(1)}, bf16[128,1152]{1,0:T(8,128)(2,1)S(1)}, bf16[128,1152]{1,0:T(8,128)(2,1)S(1)}, bf16[128,1152]{1,0:T(8,128)(2,1)S(1)}) custom-call(s32[15]{0:T(128)S(1)} %stack.55.place.which, bf16[64,8320]{1,0:T(8,128)(2,1)S(1)} %collective-permute-done.1.refs_0_, ...), custom_call_target="tpu_custom_call" | custom-call | flops 4294967296 | bytes 16777216 | tf_op jit(solution)/shard_map/score_and_deal/pallas_call | solution.py:212
  73.5 1.6 %collective-permute-start.15 = (bf16[128,1152]{1,0:T(8,128)(2,1)S(1)}, bf16[128,1152]{1,0:T(8,128)(2,1)S(1)}, u32[]{:S(2)}, u32[]{:S(2)}) collective-permute-start(bf16[128,1152]{1,0:T(8,128)(2,1)S(1)} %get-tuple-element.67), channel_id=1, source_target_pairs={{0,2},{1,3},{2,4},{3,5},{4,6},{5,7},{6,0},{7,1},{8,10},{9,11},{10,... | collective-permute-start | bytes 884744 | tf_op jit(solution)/shard_map/up_oq/ppermute | solution.py:327
  75.1 1.7 %collective-permute-start.16 = (bf16[128,1152]{1,0:T(8,128)(2,1)S(1)}, bf16[128,1152]{1,0:T(8,128)(2,1)S(1)}, u32[]{:S(2)}, u32[]{:S(2)}) collective-permute-start(bf16[128,1152]{1,0:T(8,128)(2,1)S(1)} %get-tuple-element.69), channel_id=1, source_target_pairs={{0,6},{1,7},{2,0},{3,1},{4,2},{5,3},{6,4},{7,5},{8,14},{9,15},{10,... | collective-permute-start | bytes 884744 | tf_op jit(solution)/shard_map/down_oq/ppermute | solution.py:327
  76.8 5.3 %score_group.3.refs_7_ = bf16[256,1152]{1,0:T(8,128)(2,1)S(1)} custom-call(s32[15]{0:T(128)S(1)} %stack.55.place.which, bf16[64,8320]{1,0:T(8,128)(2,1)S(1)} %collective-permute-done.refs_0_, bf16[64,8320]{1,0:T(8,128)(2,1)S(1)} %collective-permute-done.5.refs_1_, bf16[64,8320]{1,0:T(8,128)(2,1)S(1)} %collective-permute-done.8.refs_2_, ...), custom_call_target="tpu_custom_call" | custom-call | flops 4294967296 | bytes 16777216 | tf_op jit(solution)/shard_map/score_group/pallas_call | solution.py:212
  84.2 2.7 %collective-permute-start.27 = (bf16[128,1152]{1,0:T(8,128)(2,1)S(1)}, bf16[128,1152]{1,0:T(8,128)(2,1)S(1)}, u32[]{:S(2)}, u32[]{:S(2)}) collective-permute-start(bf16[128,1152]{1,0:T(8,128)(2,1)S(1)} %get-tuple-element.68), channel_id=1, source_target_pairs={{0,4},{1,5},{2,6},{3,7},{4,0},{5,1},{6,2},{7,3},{8,12},{9,13},{10,... | collective-permute-start | bytes 884744 | tf_op jit(solution)/shard_map/over_oq/ppermute | solution.py:327
  86.9 5.4 %score_and_deal.3 = (bf16[128,640]{1,0:T(8,128)(2,1)S(1)}, bf16[128,512]{1,0:T(8,128)(2,1)S(1)}, bf16[128,640]{1,0:T(8,128)(2,1)S(1)}, bf16[128,512]{1,0:T(8,128...) custom-call(s32[15]{0:T(128)S(1)} %stack.55.place.which, ...), custom_call_target="tpu_custom_call" | custom-call | flops 4294967296 | bytes 16777216 | tf_op jit(solution)/shard_map/score_and_deal/pallas_call | solution.py:212
  93.6 2.1 %collective-permute-start.20 = (bf16[128,640]{1,0:T(8,128)(2,1)S(1)}, bf16[128,640]{1,0:T(8,128)(2,1)S(1)}, u32[]{:S(2)}, u32[]{:S(2)}) collective-permute-start(bf16[128,640]{1,0:T(8,128)(2,1)S(1)} %get-tuple-element.79), channel_id=1, source_target_pairs={{0,6},{1,7},{2,0},{3,1},{4,2},{5,3},{6,4},{7,5},{8,14},{9,15},{10,... | collective-permute-start | bytes 491528 | tf_op jit(solution)/shard_map/down_st/ppermute | solution.py:327
  97.0 5.6 %collective-permute-start.28 = (bf16[128,1152]{1,0:T(8,128)(2,1)S(1)}, bf16[128,1152]{1,0:T(8,128)(2,1)S(1)}, u32[]{:S(2)}, u32[]{:S(2)}) collective-permute-start(bf16[128,1152]{1,0:T(8,128)(2,1)S(1)} %get-tuple-element.92), channel_id=1, source_target_pairs={{1,0},{2,3},{5,4},{6,7},{9,8},{10,11},{13,12},{14,15},{16,17},{19,... | collective-permute-start | bytes 884744 | tf_op jit(solution)/shard_map/oq/ppermute | solution.py:327
  102.8 3.2 %collective-permute-start.24 = (bf16[128,512]{1,0:T(8,128)(2,1)S(1)}, bf16[128,512]{1,0:T(8,128)(2,1)S(1)}, u32[]{:S(2)}, u32[]{:S(2)}) collective-permute-start(bf16[128,512]{1,0:T(8,128)(2,1)S(1)} %get-tuple-element.85), channel_id=1, source_target_pairs={{0,6},{1,7},{2,0},{3,1},{4,2},{5,3},{6,4},{7,5},{8,14},{9,15},{10,... | collective-permute-start | bytes 393224 | tf_op jit(solution)/shard_map/down_st_right/ppermute | solution.py:327
  110.5 1.9 %collective-permute-done.25.c = bf16[128,512]{1,0:T(8,128)(2,1)S(1)} collective-permute-done((bf16[128,512]{1,0:T(8,128)(2,1)S(1)}, bf16[128,512]{1,0:T(8,128)(2,1)S(1)}, u32[]{:S(2)}, u32[]{:S(2)}) %collective-permute-start.25) | collective-permute-done | bytes 131104 | tf_op jit(solution)/shard_map/over_st_right/ppermute | solution.py:327
  113.9 7.1 %collective-permute-done.26.refs_3_ = bf16[128,512]{1,0:T(8,128)(2,1)S(1)} collective-permute-done((bf16[128,512]{1,0:T(8,128)(2,1)S(1)}, bf16[128,512]{1,0:T(8,128)(2,1)S(1)}, u32[]{:S(2)}, u32[]{:S(2)}) %collective-permute-start.26) | collective-permute-done | bytes 131104 | tf_op jit(solution)/shard_map/st_right/ppermute | solution.py:327
  (52 shorter events, 16.2 us)
Async XLA Ops:
  9.3 25.3 %collective-permute-start = (bf16[64,8320]{1,0:T(8,128)(2,1)S(1)}, bf16[64,8320]{1,0:T(8,128)(2,1)S(1)}, u32[]{:S(2)}, u32[]{:S(2)}) collective-permute-start(bf16[64,8320]{1,0:T(8,128)(2,1)S(1)} %condition.1.refs_0_), channel_id=1, source_target_pairs={{0,16},{8,24},{16,0},{24,8},{32,48},{40,56},{48,32},{56,40},{64,80... | collective-permute-start | bytes 3194888 | tf_op jit(solution)/shard_map/s0/ppermute | solution.py:323
  9.7 25.7 %collective-permute-start.1 = (bf16[64,8320]{1,0:T(8,128)(2,1)S(1)}, bf16[64,8320]{1,0:T(8,128)(2,1)S(1)}, u32[]{:S(2)}, u32[]{:S(2)}) collective-permute-start(bf16[64,8320]{1,0:T(8,128)(2,1)S(1)} %condition.1.refs_0_), channel_id=1, source_target_pairs={{0,48},{8,56},{16,32},{24,40},{32,16},{40,24},{48,0},{56,8},{64,11... | collective-permute-start | bytes 3194888 | tf_op jit(solution)/shard_map/q0/ppermute | solution.py:323
  12.2 24.9 %collective-permute-start.2 = (bf16[64,8320]{1,0:T(8,128)(2,1)S(1)}, bf16[64,8320]{1,0:T(8,128)(2,1)S(1)}, u32[]{:S(2)}, u32[]{:S(2)}) collective-permute-start(bf16[64,8320]{1,0:T(8,128)(2,1)S(1)} %condition.1.refs_0_), channel_id=1, source_target_pairs={{0,64},{8,72},{16,80},{24,88},{32,96},{40,104},{48,112},{56,120},{... | collective-permute-start | bytes 3194888 | tf_op jit(solution)/shard_map/o1/ppermute | solution.py:323
  14.1 27.5 %collective-permute-start.6 = (bf16[64,8320]{1,0:T(8,128)(2,1)S(1)}, bf16[64,8320]{1,0:T(8,128)(2,1)S(1)}, u32[]{:S(2)}, u32[]{:S(2)}) collective-permute-start(bf16[64,8320]{1,0:T(8,128)(2,1)S(1)} %condition.1.refs_0_), channel_id=1, source_target_pairs={{0,8},{8,0},{16,24},{24,16},{32,40},{40,32},{48,56},{56,48},{64,72... | collective-permute-start | bytes 3194888 | tf_op jit(solution)/shard_map/own_sib/ppermute | solution.py:323
  37.0 26.6 %collective-permute-start.4 = (bf16[64,8320]{1,0:T(8,128)(2,1)S(1)}, bf16[64,8320]{1,0:T(8,128)(2,1)S(1)}, u32[]{:S(2)}, u32[]{:S(2)}) collective-permute-start(bf16[64,8320]{1,0:T(8,128)(2,1)S(1)} %collective-permute-done.2.refs_1_), channel_id=1, source_target_pairs={{0,48},{8,56},{16,32},{24,40},{32,16},{40,24},{48,0},{56,8},{64,11... | collective-permute-start | bytes 3194888 | tf_op jit(solution)/shard_map/q1/ppermute | solution.py:323
  37.3 26.3 %collective-permute-start.3 = (bf16[64,8320]{1,0:T(8,128)(2,1)S(1)}, bf16[64,8320]{1,0:T(8,128)(2,1)S(1)}, u32[]{:S(2)}, u32[]{:S(2)}) collective-permute-start(bf16[64,8320]{1,0:T(8,128)(2,1)S(1)} %collective-permute-done.1.refs_0_), channel_id=1, source_target_pairs={{0,16},{8,24},{16,0},{24,8},{32,48},{40,56},{48,32},{56,40},{64,80... | collective-permute-start | bytes 3194888 | tf_op jit(solution)/shard_map/t0/ppermute | solution.py:323
  39.7 25.5 %collective-permute-start.5 = (bf16[64,8320]{1,0:T(8,128)(2,1)S(1)}, bf16[64,8320]{1,0:T(8,128)(2,1)S(1)}, u32[]{:S(2)}, u32[]{:S(2)}) collective-permute-start(bf16[64,8320]{1,0:T(8,128)(2,1)S(1)} %collective-permute-done.refs_0_), channel_id=1, source_target_pairs={{0,64},{8,72},{16,80},{24,88},{32,96},{40,104},{48,112},{56,120},{... | collective-permute-start | bytes 3194888 | tf_op jit(solution)/shard_map/s1/ppermute | solution.py:323
  41.6 23.6 %collective-permute-start.8 = (bf16[64,8320]{1,0:T(8,128)(2,1)S(1)}, bf16[64,8320]{1,0:T(8,128)(2,1)S(1)}, u32[]{:S(2)}, u32[]{:S(2)}) collective-permute-start(bf16[64,8320]{1,0:T(8,128)(2,1)S(1)} %collective-permute-done.refs_0_), channel_id=1, source_target_pairs={{0,8},{8,0},{16,24},{24,16},{32,40},{40,32},{48,56},{56,48},{64,72... | collective-permute-start | bytes 3194888 | tf_op jit(solution)/shard_map/s0_sib/ppermute | solution.py:323
  41.6 26.0 %collective-permute-start.11 = (bf16[64,8320]{1,0:T(8,128)(2,1)S(1)}, bf16[64,8320]{1,0:T(8,128)(2,1)S(1)}, u32[]{:S(2)}, u32[]{:S(2)}) collective-permute-start(bf16[64,8320]{1,0:T(8,128)(2,1)S(1)} %collective-permute-done.1.refs_0_), channel_id=1, source_target_pairs={{0,8},{8,0},{16,24},{24,16},{32,40},{40,32},{48,56},{56,48},{64,72... | collective-permute-start | bytes 3194888 | tf_op jit(solution)/shard_map/q0_sib/ppermute | solution.py:323
  65.2 8.3 %collective-permute-start.13 = (bf16[64,8320]{1,0:T(8,128)(2,1)S(1)}, bf16[64,8320]{1,0:T(8,128)(2,1)S(1)}, u32[]{:S(2)}, u32[]{:S(2)}) collective-permute-start(bf16[64,8320]{1,0:T(8,128)(2,1)S(1)} %collective-permute-done.5.refs_1_), channel_id=1, source_target_pairs={{0,8},{8,0},{16,24},{24,16},{32,40},{40,32},{48,56},{56,48},{64,72... | collective-permute-start | bytes 3194888 | tf_op jit(solution)/shard_map/s1_sib/ppermute | solution.py:323
  65.7 7.8 %collective-permute-start.14 = (bf16[64,8320]{1,0:T(8,128)(2,1)S(1)}, bf16[64,8320]{1,0:T(8,128)(2,1)S(1)}, u32[]{:S(2)}, u32[]{:S(2)}) collective-permute-start(bf16[64,8320]{1,0:T(8,128)(2,1)S(1)} %collective-permute-done.3.b.refs_0_), channel_id=1, source_target_pairs={{0,8},{8,0},{16,24},{24,16},{32,40},{40,32},{48,56},{56,48},{64,72... | collective-permute-start | bytes 3194888 | tf_op jit(solution)/shard_map/t0_sib/ppermute | solution.py:323
  65.8 16.3 %collective-permute-start.10 = (bf16[32,8320]{1,0:T(8,128)(2,1)S(1)}, bf16[32,8320]{1,0:T(8,128)(2,1)S(1)}, u32[]{:S(2)}, u32[]{:S(2)}) collective-permute-start(bf16[32,8320]{1,0:T(8,128)(2,1)S(1)} %get-tuple-element.59), channel_id=1, source_target_pairs={{0,64},{8,72},{16,80},{24,88},{32,96},{40,104},{48,112},{56,120},{... | collective-permute-start | bytes 1597448 | tf_op jit(solution)/shard_map/t1b/ppermute | solution.py:323
  67.6 14.5 %collective-permute-start.9 = (bf16[32,8320]{1,0:T(8,128)(2,1)S(1)}, bf16[32,8320]{1,0:T(8,128)(2,1)S(1)}, u32[]{:S(2)}, u32[]{:S(2)}) collective-permute-start(bf16[32,8320]{1,0:T(8,128)(2,1)S(1)} %get-tuple-element.58), channel_id=1, source_target_pairs={{0,16},{8,24},{16,0},{24,8},{32,48},{40,56},{48,32},{56,40},{64,80... | collective-permute-start | bytes 1597448 | tf_op jit(solution)/shard_map/t1a/ppermute | solution.py:323
  73.5 10.1 %collective-permute-start.15 = (bf16[128,1152]{1,0:T(8,128)(2,1)S(1)}, bf16[128,1152]{1,0:T(8,128)(2,1)S(1)}, u32[]{:S(2)}, u32[]{:S(2)}) collective-permute-start(bf16[128,1152]{1,0:T(8,128)(2,1)S(1)} %get-tuple-element.67), channel_id=1, source_target_pairs={{0,2},{1,3},{2,4},{3,5},{4,6},{5,7},{6,0},{7,1},{8,10},{9,11},{10,... | collective-permute-start | bytes 884744 | tf_op jit(solution)/shard_map/up_oq/ppermute | solution.py:327
  75.1 8.6 %collective-permute-start.16 = (bf16[128,1152]{1,0:T(8,128)(2,1)S(1)}, bf16[128,1152]{1,0:T(8,128)(2,1)S(1)}, u32[]{:S(2)}, u32[]{:S(2)}) collective-permute-start(bf16[128,1152]{1,0:T(8,128)(2,1)S(1)} %get-tuple-element.69), channel_id=1, source_target_pairs={{0,6},{1,7},{2,0},{3,1},{4,2},{5,3},{6,4},{7,5},{8,14},{9,15},{10,... | collective-permute-start | bytes 884744 | tf_op jit(solution)/shard_map/down_oq/ppermute | solution.py:327
  84.2 12.4 %collective-permute-start.27 = (bf16[128,1152]{1,0:T(8,128)(2,1)S(1)}, bf16[128,1152]{1,0:T(8,128)(2,1)S(1)}, u32[]{:S(2)}, u32[]{:S(2)}) collective-permute-start(bf16[128,1152]{1,0:T(8,128)(2,1)S(1)} %get-tuple-element.68), channel_id=1, source_target_pairs={{0,4},{1,5},{2,6},{3,7},{4,0},{5,1},{6,2},{7,3},{8,12},{9,13},{10,... | collective-permute-start | bytes 884744 | tf_op jit(solution)/shard_map/over_oq/ppermute | solution.py:327
  92.4 10.4 %collective-permute-start.19 = (bf16[128,640]{1,0:T(8,128)(2,1)S(1)}, bf16[128,640]{1,0:T(8,128)(2,1)S(1)}, u32[]{:S(2)}, u32[]{:S(2)}) collective-permute-start(bf16[128,640]{1,0:T(8,128)(2,1)S(1)} %get-tuple-element.78), channel_id=1, source_target_pairs={{0,2},{1,3},{2,4},{3,5},{4,6},{5,7},{6,0},{7,1},{8,10},{9,11},{10,... | collective-permute-start | bytes 491528 | tf_op jit(solution)/shard_map/up_st/ppermute | solution.py:327
  93.6 12.4 %collective-permute-start.20 = (bf16[128,640]{1,0:T(8,128)(2,1)S(1)}, bf16[128,640]{1,0:T(8,128)(2,1)S(1)}, u32[]{:S(2)}, u32[]{:S(2)}) collective-permute-start(bf16[128,640]{1,0:T(8,128)(2,1)S(1)} %get-tuple-element.79), channel_id=1, source_target_pairs={{0,6},{1,7},{2,0},{3,1},{4,2},{5,3},{6,4},{7,5},{8,14},{9,15},{10,... | collective-permute-start | bytes 491528 | tf_op jit(solution)/shard_map/down_st/ppermute | solution.py:327
  95.7 11.7 %collective-permute-start.21 = (bf16[128,640]{1,0:T(8,128)(2,1)S(1)}, bf16[128,640]{1,0:T(8,128)(2,1)S(1)}, u32[]{:S(2)}, u32[]{:S(2)}) collective-permute-start(bf16[128,640]{1,0:T(8,128)(2,1)S(1)} %get-tuple-element.80), channel_id=1, source_target_pairs={{0,4},{1,5},{2,6},{3,7},{4,0},{5,1},{6,2},{7,3},{8,12},{9,13},{10,... | collective-permute-start | bytes 491528 | tf_op jit(solution)/shard_map/over_st/ppermute | solution.py:327
  97.0 16.8 %collective-permute-start.28 = (bf16[128,1152]{1,0:T(8,128)(2,1)S(1)}, bf16[128,1152]{1,0:T(8,128)(2,1)S(1)}, u32[]{:S(2)}, u32[]{:S(2)}) collective-permute-start(bf16[128,1152]{1,0:T(8,128)(2,1)S(1)} %get-tuple-element.92), channel_id=1, source_target_pairs={{1,0},{2,3},{5,4},{6,7},{9,8},{10,11},{13,12},{14,15},{16,17},{19,... | collective-permute-start | bytes 884744 | tf_op jit(solution)/shard_map/oq/ppermute | solution.py:327
  102.7 7.7 %collective-permute-start.23 = (bf16[128,512]{1,0:T(8,128)(2,1)S(1)}, bf16[128,512]{1,0:T(8,128)(2,1)S(1)}, u32[]{:S(2)}, u32[]{:S(2)}) collective-permute-start(bf16[128,512]{1,0:T(8,128)(2,1)S(1)} %get-tuple-element.84), channel_id=1, source_target_pairs={{0,2},{1,3},{2,4},{3,5},{4,6},{5,7},{6,0},{7,1},{8,10},{9,11},{10,... | collective-permute-start | bytes 393224 | tf_op jit(solution)/shard_map/up_st_right/ppermute | solution.py:327
  102.8 7.8 %collective-permute-start.24 = (bf16[128,512]{1,0:T(8,128)(2,1)S(1)}, bf16[128,512]{1,0:T(8,128)(2,1)S(1)}, u32[]{:S(2)}, u32[]{:S(2)}) collective-permute-start(bf16[128,512]{1,0:T(8,128)(2,1)S(1)} %get-tuple-element.85), channel_id=1, source_target_pairs={{0,6},{1,7},{2,0},{3,1},{4,2},{5,3},{6,4},{7,5},{8,14},{9,15},{10,... | collective-permute-start | bytes 393224 | tf_op jit(solution)/shard_map/down_st_right/ppermute | solution.py:327
  107.6 13.3 %collective-permute-start.22 = (bf16[128,640]{1,0:T(8,128)(2,1)S(1)}, bf16[128,640]{1,0:T(8,128)(2,1)S(1)}, u32[]{:S(2)}, u32[]{:S(2)}) collective-permute-start(bf16[128,640]{1,0:T(8,128)(2,1)S(1)} %get-tuple-element.82), channel_id=1, source_target_pairs={{0,1},{3,2},{4,5},{7,6},{8,9},{11,10},{12,13},{15,14},{17,16},{18,... | collective-permute-start | bytes 491528 | tf_op jit(solution)/shard_map/st/ppermute | solution.py:327
  112.5 8.4 %collective-permute-start.26 = (bf16[128,512]{1,0:T(8,128)(2,1)S(1)}, bf16[128,512]{1,0:T(8,128)(2,1)S(1)}, u32[]{:S(2)}, u32[]{:S(2)}) collective-permute-start(bf16[128,512]{1,0:T(8,128)(2,1)S(1)} %get-tuple-element.88), channel_id=1, source_target_pairs={{0,1},{3,2},{4,5},{7,6},{8,9},{11,10},{12,13},{15,14},{17,16},{18,... | collective-permute-start | bytes 393224 | tf_op jit(solution)/shard_map/st_right/ppermute | solution.py:327
  (7 other events, 22.1 us)
